TPU v7x, 256 devices: a whole 4x4x8 slice. The times are simulated.
256 devices in a mesh: blk: 32 (over y, x, core), grp: 8 (over z).
Axes of the slice: x: 4, y: 4, z: 8, core: 2. Of those that a mesh axis runs over, the one named last changes fastest.
Arguments:
- rhs: float32 [7, 262144], P(None, ('blk', 'grp')), may hold values from -36 to 36
- diag_blocks: float32 [7, 7, 262144], P(None, None, ('blk', 'grp'))
- lower_blocks: float32 [7, 7, 262144], P(None, None, ('blk', 'grp')), may hold values from -1.5 to 1.5
- upper_blocks: float32 [7, 7, 262144], P(None, None, ('blk', 'grp')), may hold values from -1.5 to 1.5
- precond: float32 [7, 7, 262144], P(None, None, ('blk', 'grp'))
- coupling: float32 [256, 7, 7, 32, 128], P(('blk', 'grp')), may hold values from -1.5 to 1.5
- send_cells: int32 [256, 32, 128], P(('blk', 'grp')), may hold values from 0 to 1023
- recv_cells: int32 [256, 32, 128], P(('blk', 'grp')), may hold values from 0 to 1023
- halo_len: int32 [256, 32], P(('blk', 'grp')), may hold values from 0 to 128, as said below
Outputs:
- adjoint: float32 [7, 262144], P(None, ('blk', 'grp'))
- residual: float32 [7, 262144], P(None, ('blk', 'grp'))
Inputs may be any that keep to these rules, and one draw needn't show every extreme that they name: `halo_len`: every device has at least one peer with exactly 128 face cells.
All inputs are finite; a program needn't handle non-finite values.
Results may differ from a plain program's by a relative error of at most 0.0013.
Values sent between devices are 32-bit elements; how exact they have to be, the bound alone decides.
No kernel may reach another device: no remote copies, remote signals or barrier semaphores. Data moves between devices by JAX's collectives and lax.ppermute only.
A program may use at most 128 MiB of HBM per device.

v0:
```python
import jax
import jax.numpy as jnp
from jax import lax
from jax.sharding import PartitionSpec as P

ITERS = 4


def mixing(blocks, field):
    total = blocks[:, 0] * field[0][None]
    for inner in range(1, field.shape[0]):
        total = total + blocks[:, inner] * field[inner][None]
    return total


def operate(field, diag_blocks, lower_blocks, upper_blocks, couple_used, send_flat, recv_flat):
    fields = field.shape[0]
    peers = couple_used.shape[2]
    width = couple_used.shape[3]
    zero_col = jnp.zeros((fields, 1), jnp.float32)
    before = jnp.concatenate([zero_col, field[:, :-1]], axis=1)
    after = jnp.concatenate([field[:, 1:], zero_col], axis=1)
    outgoing = jnp.take(field, send_flat, axis=1).reshape(fields, peers, width)
    incoming = lax.all_to_all(outgoing, "blk", split_axis=1, concat_axis=1, tiled=True)
    term = mixing(couple_used, incoming)
    local = mixing(diag_blocks, field) + mixing(lower_blocks, before) + mixing(upper_blocks, after)
    return local.at[:, recv_flat].add(term.reshape(fields, -1))


def per_device(
    rhs,
    diag_blocks,
    lower_blocks,
    upper_blocks,
    precond,
    coupling,
    send_cells,
    recv_cells,
    halo_len,
):
    width = coupling.shape[4]
    slots = jnp.arange(width, dtype=jnp.int32)
    live = (slots[None, :] < halo_len[0][:, None]).astype(jnp.float32)
    masked = coupling[0] * live[None, None, :, :]
    couple_used = lax.all_to_all(masked, "blk", split_axis=2, concat_axis=2, tiled=True)
    send_flat = send_cells[0].reshape(-1)
    recv_flat = recv_cells[0].reshape(-1)

    def apply_op(field):
        return operate(
            field, diag_blocks, lower_blocks, upper_blocks, couple_used, send_flat, recv_flat
        )

    beta = jnp.sqrt(lax.psum(jnp.sum(rhs * rhs), ("blk", "grp")))
    basis = [rhs / beta]
    hess = jnp.zeros((ITERS + 1, ITERS), jnp.float32)
    for col in range(ITERS):
        product = apply_op(mixing(precond, basis[col]))
        local_proj = jnp.stack([jnp.sum(vector * product) for vector in basis])
        proj = lax.psum(local_proj, ("blk", "grp"))
        remain = product
        for index in range(col + 1):
            remain = remain - proj[index] * basis[index]
        height = jnp.sqrt(lax.psum(jnp.sum(remain * remain), ("blk", "grp")))
        hess = hess.at[: col + 1, col].set(proj).at[col + 1, col].set(height)
        basis.append(remain / height)
    gram = jnp.dot(hess.T, hess, precision=lax.Precision.HIGHEST)
    factor = jnp.linalg.cholesky(gram)
    coef = jax.scipy.linalg.cho_solve((factor, True), beta * hess[0])
    combo = coef[0] * basis[0]
    for index in range(1, ITERS):
        combo = combo + coef[index] * basis[index]
    adjoint = mixing(precond, combo)
    residual = rhs - apply_op(adjoint)
    return (adjoint, residual)


def solution(mesh):
    return jax.shard_map(
        per_device,
        mesh=mesh,
        in_specs=(
            P(None, ("blk", "grp")),
            P(None, None, ("blk", "grp")),
            P(None, None, ("blk", "grp")),
            P(None, None, ("blk", "grp")),
            P(None, None, ("blk", "grp")),
            P(("blk", "grp"), None, None, None, None),
            P(("blk", "grp"), None, None),
            P(("blk", "grp"), None, None),
            P(("blk", "grp"), None),
        ),
        out_specs=(P(None, ("blk", "grp")), P(None, ("blk", "grp"))),
        check_vma=False,
    )
```

profile of v0, /device:TPU:1, one launch (start us, length us, event | category | flops | bytes accessed | tf_op | source)
XLA Modules:
  0.0 1161.7 jit_solution(11489041085819217545)
XLA Ops:
  10.4 81.4 %psum.63 = f32[]{:T(128)} all-reduce(f32[]{:T(128)} %multiply_reduce_fusion.14), channel_id=1, replica_groups=mesh['blk'=32,'grp'=8] {'blk','grp'}, use_global_device_ids=true, to_apply=%region_1.0 | all-reduce | flops 1 | bytes 8 | tf_op jit(solution)/shard_map/psum | solution.py:54
  95.7 14.1 %gather_fusion = f32[4096,7]{1,0:T(8,128)} fusion(f32[7,1024]{0,1:T(8,128)S(1)} %fusion.100, s32[4096]{0:T(1024)S(1)} %fusion.166), kind=kCustom, calls=%fused_computation.clone | custom fusion | bytes 245760 | tf_op jit(solution)/shard_map/jit(_take)/gather | solution.py:23
  133.2 8.0 all-to-all-start
  163.1 7.7 fusion.1
  180.2 22.9 %scatter_fusion = f32[7,1024]{0,1:T(8,128)S(1)} fusion(f32[7,1024]{0,1:T(8,128)S(1)} %fusion.1, s32[4096]{0:T(1024)S(1)} %bitcast.1105, f32[4096,7]{1,0:T(8,128)} %copy.274), kind=kCustom, calls=%fused_computation.5 | custom fusion | flops 28672 | bytes 360448 | tf_op jit(solution)/shard_map/scatter-add | solution.py:27
  203.9 75.7 %psum.64 = f32[1]{0:T(128)} all-reduce(f32[1]{0:T(128)} %bitcast.43), channel_id=1, replica_groups=mesh['blk'=32,'grp'=8] {'blk','grp'}, use_global_device_ids=true, to_apply=%region_4.6 | all-reduce | flops 1 | bytes 8 | tf_op jit(solution)/shard_map/psum | solution.py:60
  281.6 73.6 %psum.65 = f32[]{:T(128)} all-reduce(f32[]{:T(128)} %multiply_reduce_fusion.12), channel_id=1, replica_groups=mesh['blk'=32,'grp'=8] {'blk','grp'}, use_global_device_ids=true, to_apply=%region_6.8 | all-reduce | flops 1 | bytes 8 | tf_op jit(solution)/shard_map/psum | solution.py:64
  363.0 14.1 %gather_fusion.1 = f32[4096,7]{1,0:T(8,128)} fusion(f32[7,1024]{0,1:T(8,128)S(1)} %fusion.101, s32[4096]{0:T(1024)S(1)} %fusion.166), kind=kCustom, calls=%fused_computation.1.clone | custom fusion | bytes 245760 | tf_op jit(solution)/shard_map/jit(_take)/gather | solution.py:23
  377.1 4.9 slice_reduce_fusion.118
  397.0 8.4 fusion.3
  411.1 22.9 %scatter_fusion.1 = f32[7,1024]{0,1:T(8,128)S(1)} fusion(f32[7,1024]{0,1:T(8,128)S(1)} %copy-done.35, s32[4096]{0:T(1024)S(1)} %bitcast.1106, f32[4096,7]{1,0:T(8,128)} %copy.283), kind=kCustom, calls=%fused_computation.6 | custom fusion | flops 28672 | bytes 360448 | tf_op jit(solution)/shard_map/scatter-add | solution.py:27
  436.3 75.9 %psum.66 = f32[2]{0:T(128)S(1)} all-reduce(f32[2]{0:T(128)S(1)} %pad_maximum_fusion), channel_id=1, replica_groups=mesh['blk'=32,'grp'=8] {'blk','grp'}, use_global_device_ids=true, to_apply=%region_11.13 | all-reduce | flops 2 | bytes 16 | tf_op jit(solution)/shard_map/psum | solution.py:60
  514.7 73.8 %psum.67 = f32[]{:T(128)} all-reduce(f32[]{:T(128)} %get-tuple-element.258), channel_id=1, replica_groups=mesh['blk'=32,'grp'=8] {'blk','grp'}, use_global_device_ids=true, to_apply=%region_13.15 | all-reduce | flops 1 | bytes 8 | tf_op jit(solution)/shard_map/psum | solution.py:64
  596.1 14.1 %gather_fusion.2 = f32[4096,7]{1,0:T(8,128)} fusion(f32[7,1024]{0,1:T(8,128)S(1)} %fusion.102, s32[4096]{0:T(1024)S(1)} %fusion.166), kind=kCustom, calls=%fused_computation.2.clone | custom fusion | bytes 245760 | tf_op jit(solution)/shard_map/jit(_take)/gather | solution.py:23
  610.2 5.1 slice_reduce_fusion.104
  615.3 5.5 slice_reduce_fusion.111
  633.3 8.5 fusion.5
  651.9 23.0 %scatter_fusion.2 = f32[7,1024]{0,1:T(8,128)S(1)} fusion(f32[7,1024]{0,1:T(8,128)S(1)} %copy-done.36, s32[4096]{0:T(1024)S(1)} %bitcast.1107, f32[4096,7]{1,0:T(8,128)} %copy.292), kind=kCustom, calls=%fused_computation.7 | custom fusion | flops 28672 | bytes 360448 | tf_op jit(solution)/shard_map/scatter-add | solution.py:27
  677.8 75.9 %psum.68 = f32[3]{0:T(128)S(1)} all-reduce(f32[3]{0:T(128)S(1)} %pad_maximum_fusion.1), channel_id=1, replica_groups=mesh['blk'=32,'grp'=8] {'blk','grp'}, use_global_device_ids=true, to_apply=%region_19.21 | all-reduce | flops 3 | bytes 24 | tf_op jit(solution)/shard_map/psum | solution.py:60
  757.9 73.4 %psum.69 = f32[]{:T(128)} all-reduce(f32[]{:T(128)} %get-tuple-element.256), channel_id=1, replica_groups=mesh['blk'=32,'grp'=8] {'blk','grp'}, use_global_device_ids=true, to_apply=%region_21.23 | all-reduce | flops 1 | bytes 8 | tf_op jit(solution)/shard_map/psum | solution.py:64
  838.9 14.1 %gather_fusion.3 = f32[4096,7]{1,0:T(8,128)} fusion(f32[7,1024]{0,1:T(8,128)S(1)} %fusion.103, s32[4096]{0:T(1024)S(1)} %fusion.166), kind=kCustom, calls=%fused_computation.3.clone | custom fusion | bytes 245760 | tf_op jit(solution)/shard_map/jit(_take)/gather | solution.py:23
  852.9 5.2 slice_reduce_fusion.90
  858.1 5.2 slice_reduce_fusion.97
  870.9 5.2 all-to-all-start.4
  876.2 8.5 fusion.7
  894.7 22.2 %scatter_fusion.3 = f32[7,1024]{0,1:T(8,128)} fusion(f32[7,1024]{0,1:T(8,128)} %fusion.7, s32[4096]{0:T(1024)S(1)} %bitcast.1108, f32[4096,7]{1,0:T(8,128)} %copy.301), kind=kCustom, calls=%fused_computation.8 | custom fusion | flops 28672 | bytes 360448 | tf_op jit(solution)/shard_map/scatter-add | solution.py:27
  921.7 76.0 %psum.70 = f32[4]{0:T(128)S(1)} all-reduce(f32[4]{0:T(128)S(1)} %pad_maximum_fusion.2), channel_id=1, replica_groups=mesh['blk'=32,'grp'=8] {'blk','grp'}, use_global_device_ids=true, to_apply=%region_28.30 | all-reduce | flops 4 | bytes 32 | tf_op jit(solution)/shard_map/psum | solution.py:60
  1006.1 73.4 %psum.71 = f32[]{:T(128)} all-reduce(f32[]{:T(128)} %multiply_reduce_fusion), channel_id=1, replica_groups=mesh['blk'=32,'grp'=8] {'blk','grp'}, use_global_device_ids=true, to_apply=%region_30.32 | all-reduce | flops 1 | bytes 8 | tf_op jit(solution)/shard_map/psum | solution.py:64
  1092.4 14.1 %gather_fusion.4 = f32[4096,7]{1,0:T(8,128)} fusion(f32[7,1024]{0,1:T(8,128)S(1)} %fusion.104, s32[4096]{0:T(1024)S(1)} %fusion.166), kind=kCustom, calls=%fused_computation.4.clone | custom fusion | bytes 245760 | tf_op jit(solution)/shard_map/jit(_take)/gather | solution.py:23
  1118.5 4.8 all-to-all-start.5
  1123.4 8.2 fusion.9
  1137.5 22.9 %scatter_fusion.4 = f32[7,1024]{0,1:T(8,128)S(1)} fusion(f32[7,1024]{0,1:T(8,128)S(1)} %copy-done.38, s32[4096]{0:T(1024)S(1)} %bitcast.1109, f32[4096,7]{1,0:T(8,128)} %copy.312), kind=kCustom, calls=%fused_computation.9 | custom fusion | flops 28672 | bytes 360448 | tf_op jit(solution)/shard_map/scatter-add | solution.py:27
  (272 shorter events, 207.4 us)
Async XLA Ops:
  7.0 351.4 %copy-start = (f32[7,1,1024]{0,2,1:T(8,128)}, f32[7,1,1024]{0,2,1:T(8,128)S(1)}, u32[]{:S(2)}) copy-start(f32[7,1,1024]{0,2,1:T(8,128)S(1)} %copy.321) | copy-start | bytes 86020
  7.2 87.1 %copy-start.4 = (f32[7,1,1024]{0,2,1:T(8,128)}, f32[7,1,1024]{0,2,1:T(8,128)S(1)}, u32[]{:S(2)}) copy-start(f32[7,1,1024]{0,2,1:T(8,128)S(1)} %copy.320) | copy-start | bytes 86020
  117.4 15.8 %all-to-all-start.1 = ((f32[7,32,128]{2,0,1:T(8,128)}), f32[7,32,128]{2,0,1:T(8,128)S(1)}, u32[]{:S(2)}, u32[]{:S(2)}) async-start(f32[7,32,128]{2,0,1:T(8,128)} %copy.260), calls=%async_computation.1 | async-start | bytes 262144 | tf_op jit(solution)/shard_map/all_to_all | solution.py:24
  124.4 7.4 copy-start.43
  133.2 38.3 %all-to-all-start = ((f32[7,7,32,128]{3,1,0,2:T(8,128)}), f32[7,7,32,128]{3,1,0,2:T(8,128)}, u32[]{:S(2)}, u32[]{:S(2)}) async-start(f32[7,7,32,128]{3,1,0,2:T(8,128)} %bitcast_multiply_fusion), calls=%async_computation | async-start | bytes 1835008 | tf_op jit(solution)/shard_map/all_to_all | solution.py:45
  142.1 21.0 %copy-start.24 = (f32[7,1,1024]{0,2,1:T(8,128)}, f32[7,1,1024]{0,2,1:T(8,128)S(1)}, u32[]{:S(2)}) copy-start(f32[7,1,1024]{0,2,1:T(8,128)S(1)} %copy.343) | copy-start | bytes 86020
  176.1 27.0 %copy-start.39 = (f32[1,7,32,128]{3,2,1,0:T(8,128)}, f32[1,7,32,128]{3,2,1,0:T(8,128)S(1)}, u32[]{:S(2)}) copy-start(f32[1,7,32,128]{3,2,1,0:T(8,128)S(1)} %get-tuple-element.368) | copy-start | bytes 344068
  176.1 27.0 %copy-start.40 = (f32[1,7,32,128]{3,2,1,0:T(8,128)}, f32[1,7,32,128]{3,2,1,0:T(8,128)S(1)}, u32[]{:S(2)}) copy-start(f32[1,7,32,128]{3,2,1,0:T(8,128)S(1)} %get-tuple-element.369) | copy-start | bytes 344068
  176.1 27.0 %copy-start.41 = (f32[1,7,32,128]{3,2,1,0:T(8,128)}, f32[1,7,32,128]{3,2,1,0:T(8,128)S(1)}, u32[]{:S(2)}) copy-start(f32[1,7,32,128]{3,2,1,0:T(8,128)S(1)} %get-tuple-element.370) | copy-start | bytes 344068
  176.1 27.0 %copy-start.42 = (f32[1,7,32,128]{3,2,1,0:T(8,128)}, f32[1,7,32,128]{3,2,1,0:T(8,128)S(1)}, u32[]{:S(2)}) copy-start(f32[1,7,32,128]{3,2,1,0:T(8,128)S(1)} %get-tuple-element.371) | copy-start | bytes 344068
  389.2 7.8 copy-start.25
  389.2 7.8 copy-start.29
  392.1 13.9 %all-to-all-start.2 = ((f32[7,32,128]{2,0,1:T(8,128)}), f32[7,32,128]{2,0,1:T(8,128)}, u32[]{:S(2)}, u32[]{:S(2)}) async-start(f32[7,32,128]{2,0,1:T(8,128)} %copy.275), calls=%async_computation.2 | async-start | bytes 262144 | tf_op jit(solution)/shard_map/all_to_all | solution.py:24
  405.4 5.7 copy-start.35
  625.5 7.7 copy-start.26
  628.4 16.8 %all-to-all-start.3 = ((f32[7,32,128]{2,0,1:T(8,128)}), f32[7,32,128]{2,0,1:T(8,128)}, u32[]{:S(2)}, u32[]{:S(2)}) async-start(f32[7,32,128]{2,0,1:T(8,128)} %copy.284), calls=%async_computation.3 | async-start | bytes 262144 | tf_op jit(solution)/shard_map/all_to_all | solution.py:24
  633.3 8.5 copy-start.54
  641.8 10.1 copy-start.36
  674.9 79.3 %copy-start.37 = (f32[7,1024]{0,1:T(8,128)}, f32[7,1024]{0,1:T(8,128)S(1)}, u32[]{:S(2)}) copy-start(f32[7,1024]{0,1:T(8,128)S(1)} %scatter_fusion.2) | copy-start | bytes 86020
  753.7 80.3 %copy-start.51 = (f32[3]{0:T(128)}, f32[3]{0:T(128)S(1)}, u32[]{:S(2)}) copy-start(f32[3]{0:T(128)S(1)} %psum.68) | copy-start | bytes 40
  757.9 76.1 %copy-start.33 = (f32[7,1024]{0,1:T(8,128)}, f32[7,1024]{0,1:T(8,128)S(1)}, u32[]{:S(2)}) copy-start(f32[7,1024]{0,1:T(8,128)S(1)} %get-tuple-element.257) | copy-start | bytes 86020
  868.0 8.1 copy-start.27
  870.9 17.1 %all-to-all-start.4 = ((f32[7,32,128]{2,0,1:T(8,128)}), f32[7,32,128]{2,0,1:T(8,128)}, u32[]{:S(2)}, u32[]{:S(2)}) async-start(f32[7,32,128]{2,0,1:T(8,128)} %copy.293), calls=%async_computation.4 | async-start | bytes 262144 | tf_op jit(solution)/shard_map/all_to_all | solution.py:24
  876.2 8.5 copy-start.52
  891.8 25.2 %copy-start.34 = (f32[7,1024]{0,1:T(8,128)S(1)}, f32[7,1024]{0,1:T(8,128)}, u32[]{:S(2)}) copy-start(f32[7,1024]{0,1:T(8,128)} %copy-done.33) | copy-start | bytes 86020
  1115.5 7.9 copy-start.28
  1115.5 7.9 copy-start.30
  1115.5 7.9 copy-start.31
  1115.5 7.9 copy-start.32
  1115.5 7.9 copy-start.49
  1118.5 13.9 %all-to-all-start.5 = ((f32[7,32,128]{2,0,1:T(8,128)}), f32[7,32,128]{2,0,1:T(8,128)}, u32[]{:S(2)}, u32[]{:S(2)}) async-start(f32[7,32,128]{2,0,1:T(8,128)} %copy.304), calls=%async_computation.5 | async-start | bytes 262144 | tf_op jit(solution)/shard_map/all_to_all | solution.py:24
  1131.6 5.9 copy-start.38
  (32 other events, 74.4 us)
where the time goes:
time: 1180 us; the launch traced here: 1160 us
  blocking collectives  679 us (58%)
  other arithmetic  234 us (20%)
  local copies, waits for them, and re-layouts  211 us (18%)
  starting transfers between devices  32.1 us (3%)
    psum x4, blocking collectives, per_device(): proj = lax.psum(local_proj, ('blk', 'grp'))  303 us
    psum x4, blocking collectives, per_device(): height = jnp.sqrt(lax.psum(jnp.sum(remain * remain), ('blk', 'grp')))  294 us
    scatter-add x5, other arithmetic, operate(): return local.at[:, recv_flat].add(term.reshape(fields, -1))  114 us
    psum x1, blocking collectives, per_device(): beta = jnp.sqrt(lax.psum(jnp.sum(rhs * rhs), ('blk', 'grp')))  81.4 us
    slice x30, local copies, waits for them, and re-layouts, mixing(): total = blocks[:, 0] * field[0][None]  71.8 us
    gather x5, local copies, waits for them, and re-layouts, operate(): outgoing = jnp.take(field, send_flat, axis=1).reshape(fields, peers, width)  70.4 us
    add x5, other arithmetic, operate(): mixing(diag_blocks, field) + mixing(lower_blocks, before)  41.4 us
    unnamed x150, local copies, waits for them, and re-layouts  28 us
  transfers between devices with their start and end apart: 6, of which 0 were waited for; matrix products, arithmetic and copies ran while one was open for 7% of the time, Pallas kernels for 0%

commit v1 on v0

v1 whole, which is shorter than its diff:
```python
import functools

import jax
import jax.numpy as jnp
from jax import lax
from jax.experimental import pallas as pl
from jax.experimental.pallas import tpu as pltpu
from jax.sharding import PartitionSpec as P

ITERS = 4
F = 7
LANES = 128
BOTH = ("blk", "grp")


def mixing(blocks, field):
    total = blocks[:, 0] * field[0][None]
    for inner in range(1, field.shape[0]):
        total = total + blocks[:, inner] * field[inner][None]
    return total


def operate(field, diag_blocks, lower_blocks, upper_blocks, masked, send_flat, recv_flat):
    fields = field.shape[0]
    peers, width = masked.shape[2:]
    zero_col = jnp.zeros((fields, 1), jnp.float32)
    before = jnp.concatenate([zero_col, field[:, :-1]], axis=1)
    after = jnp.concatenate([field[:, 1:], zero_col], axis=1)
    outgoing = jnp.take(field, send_flat, axis=1).reshape(fields, peers, width)
    term = lax.all_to_all(mixing(masked, outgoing), "blk", split_axis=1, concat_axis=1, tiled=True)
    local = mixing(diag_blocks, field) + mixing(lower_blocks, before) + mixing(upper_blocks, after)
    return local.at[:, recv_flat].add(term.reshape(fields, -1))


def arnoldi(rhs, diag_blocks, lower_blocks, upper_blocks, precond, coupling, send_cells, recv_cells, halo_len):
    slots = jnp.arange(coupling.shape[4], dtype=jnp.int32)
    live = (slots[None, :] < halo_len[0][:, None]).astype(jnp.float32)
    masked = coupling[0] * live[None, None, :, :]
    send_flat = send_cells[0].reshape(-1)
    recv_flat = recv_cells[0].reshape(-1)

    def apply_op(field):
        return operate(field, diag_blocks, lower_blocks, upper_blocks, masked, send_flat, recv_flat)

    beta = jnp.sqrt(lax.psum(jnp.sum(rhs * rhs), BOTH))
    basis = [rhs / beta]
    hess = jnp.zeros((ITERS + 1, ITERS), jnp.float32)
    for col in range(ITERS):
        product = apply_op(mixing(precond, basis[col]))
        proj = lax.psum(jnp.stack([jnp.sum(vector * product) for vector in basis]), BOTH)
        remain = product
        for index in range(col + 1):
            remain = remain - proj[index] * basis[index]
        height = jnp.sqrt(lax.psum(jnp.sum(remain * remain), BOTH))
        hess = hess.at[: col + 1, col].set(proj).at[col + 1, col].set(height)
        basis.append(remain / height)
    gram = jnp.dot(hess.T, hess, precision=lax.Precision.HIGHEST)
    factor = jnp.linalg.cholesky(gram)
    coef = jax.scipy.linalg.cho_solve((factor, True), beta * hess[0])
    combo = coef[0] * basis[0]
    for index in range(1, ITERS):
        combo = combo + coef[index] * basis[index]
    adjoint = mixing(precond, combo)
    return adjoint, rhs - apply_op(adjoint)


def two_sum(a, b):
    s = a + b
    t = s - a
    return s, (a - (s - t)) + (b - t)


def quick_sum(a, b):
    s = a + b
    return s, b - (s - a)


def halves(a):
    t = a * 4097.0
    high = t - (t - a)
    return high, a - high


def two_prod(a, ah, al, b, bh, bl):
    p = a * b
    return p, ((ah * bh - p) + ah * bl + al * bh) + al * bl


def dd_add(a, b):
    s, e = two_sum(a[0], b[0])
    return quick_sum(s, e + (a[1] + b[1]))


def dd_mul(a, b):
    p, e = two_prod(a[0], *halves(a[0]), b[0], *halves(b[0]))
    return quick_sum(p, e + (a[0] * b[1] + a[1] * b[0]))


def dd_neg(a):
    return -a[0], -a[1]


def dd_div(a, b):
    q = a[0] / b[0]
    rest = dd_add(a, dd_neg(dd_mul(b, (q, jnp.zeros_like(q)))))
    return quick_sum(q, rest[0] / b[0])


def row_sums(parts):
    rows = [jnp.sum(part, axis=0, keepdims=True) for part in parts]
    return jnp.concatenate(rows + [jnp.zeros_like(rows[0])], axis=0)


def precondition(pre_ref, u):
    return row_sums([pre_ref[i] * u[:F] for i in range(F)])


def write_message(z, coup_ref, send_ref, halo_ref, msg_ref):
    cells = z.shape[1]
    tiles = cells // LANES
    peers = send_ref.shape[1]
    source = [
        [jnp.broadcast_to(z[f : f + 1, t * LANES : (t + 1) * LANES], (8, LANES)) for t in range(tiles)]
        for f in range(F)
    ]
    lanes = lax.broadcasted_iota(jnp.int32, (8, LANES), 1)
    rows = lax.broadcasted_iota(jnp.int32, (8, peers), 0)
    cols = lax.broadcasted_iota(jnp.int32, (8, peers), 1)
    lens = jnp.broadcast_to(halo_ref[...], (8, peers))
    for q in range(peers // 8):
        cell = send_ref[0, q * 8 : (q + 1) * 8, :]
        low = cell & (LANES - 1)
        high = cell >> 7
        size = jnp.sum(jnp.where(cols == rows + q * 8, lens, 0), axis=1, keepdims=True)
        live = lanes < size
        taken = []
        for f in range(F):
            got = jnp.take_along_axis(source[f][0], low, axis=1, mode="promise_in_bounds")
            for t in range(1, tiles):
                other = jnp.take_along_axis(source[f][t], low, axis=1, mode="promise_in_bounds")
                got = jnp.where(high == t, other, got)
            taken.append(got)
        for i in range(F):
            total = coup_ref[0, i, 0, q * 8 : (q + 1) * 8, :] * taken[0]
            for j in range(1, F):
                total = total + coup_ref[0, i, j, q * 8 : (q + 1) * 8, :] * taken[j]
            msg_ref[pl.ds(q * 64 + i, 8, stride=8), :] = jnp.where(live, total, 0.0)
        msg_ref[pl.ds(q * 64 + F, 8, stride=8), :] = jnp.zeros((8, LANES), jnp.float32)


def scatter(recv_ref, cells_ref, tiles):
    peers = cells_ref.shape[1]
    spots = lax.broadcasted_iota(jnp.int32, (LANES, LANES), 0)
    left, right = [], []
    for s in range(peers):
        x = recv_ref[s * 8 : (s + 1) * 8, :]
        first = x.astype(jnp.bfloat16).astype(jnp.float32)
        rest = x - first
        second = rest.astype(jnp.bfloat16).astype(jnp.float32)
        third = rest - second
        cell = cells_ref[0, s : s + 1, :]
        low = jnp.broadcast_to(cell & (LANES - 1), (LANES, LANES))
        high = jnp.broadcast_to(cell >> 7, (8, LANES))
        pieces = []
        for t in range(tiles):
            here = high == t
            pieces += [jnp.where(here, part, 0.0) for part in (first, second, third)]
        left.append(jnp.concatenate(pieces, axis=0).astype(jnp.bfloat16))
        right.append(jnp.where(spots == low, 1.0, 0.0).astype(jnp.bfloat16))
    total = lax.dot_general(
        jnp.concatenate(left, axis=1),
        jnp.concatenate(right, axis=1),
        (((1,), (1,)), ((), ())),
        preferred_element_type=jnp.float32,
    )
    out = []
    for t in range(tiles):
        a, b, c = (total[t * 24 + 8 * k : t * 24 + 8 * k + 8] for k in range(3))
        out.append((c + b) + a)
    return jnp.concatenate(out, axis=1)


def products(us, last):
    cells = last.shape[1]
    tiles = [slice(t * LANES, (t + 1) * LANES) for t in range(cells // LANES)]
    lh, ll = halves(last)
    rows = lax.broadcasted_iota(jnp.int32, (8, LANES), 0)
    hi = jnp.zeros((8, LANES), jnp.float32)
    lo = jnp.zeros((8, LANES), jnp.float32)
    for i, u in enumerate(us):
        uh, ul = halves(u)
        terms = []
        for t in tiles:
            terms.append(two_prod(u[:, t], uh[:, t], ul[:, t], last[:, t], lh[:, t], ll[:, t]))
        while len(terms) > 1:
            terms = [dd_add(terms[k], terms[k + 1]) for k in range(0, len(terms), 2)]
        total = terms[0]
        for shift in (4, 2, 1):
            total = dd_add(total, tuple(pltpu.roll(v, shift, 0) for v in total))
        hi = jnp.where(rows == i, total[0], hi)
        lo = jnp.where(rows == i, total[1], lo)
    total = (hi, lo)
    for shift in (64, 32, 16, 8, 4, 2, 1):
        total = dd_add(total, tuple(pltpu.roll(v, shift, 1) for v in total))
    return total


def first_kernel(rhs_ref, pre_ref, coup_ref, send_ref, halo_ref, u_ref, z_ref, msg_ref):
    u = jnp.concatenate([rhs_ref[...], jnp.zeros((1, rhs_ref.shape[1]), jnp.float32)], axis=0)
    z = precondition(pre_ref, u)
    u_ref[...] = u
    z_ref[...] = z
    write_message(z, coup_ref, send_ref, halo_ref, msg_ref)


def local_kernel(count, z_ref, diag_ref, low_ref, up_ref, *refs):
    u_refs, (y_ref, gram_ref) = refs[:count], refs[count:]
    z = z_ref[...]
    cells = z.shape[1]
    col = lax.broadcasted_iota(jnp.int32, z.shape, 1)
    before = jnp.where(col == 0, 0.0, pltpu.roll(z, 1, 1))[:F]
    after = jnp.where(col == cells - 1, 0.0, pltpu.roll(z, cells - 1, 1))[:F]
    z = z[:F]
    y_ref[...] = row_sums([diag_ref[i] * z + low_ref[i] * before + up_ref[i] * after for i in range(F)])
    us = [ref[...] for ref in u_refs]
    gram_ref[0], gram_ref[1] = products(us, us[-1])


def step_kernel(recv_ref, cells_ref, y_ref, pre_ref, coup_ref, send_ref, halo_ref, u_ref, z_ref, msg_ref):
    u = y_ref[...] + scatter(recv_ref, cells_ref, y_ref.shape[1] // LANES)
    z = precondition(pre_ref, u)
    u_ref[...] = u
    z_ref[...] = z
    write_message(z, coup_ref, send_ref, halo_ref, msg_ref)


def last_kernel(recv_ref, cells_ref, y_ref, *refs):
    u_refs, gram_refs, (u_ref, msg_ref) = refs[:ITERS], refs[ITERS : 2 * ITERS], refs[2 * ITERS :]
    u = y_ref[...] + scatter(recv_ref, cells_ref, y_ref.shape[1] // LANES)
    u_ref[...] = u
    columns = [(ref[0], ref[1]) for ref in gram_refs]
    columns.append(products([ref[...] for ref in u_refs] + [u], u))
    lane = lax.broadcasted_iota(jnp.int32, (1, LANES), 1)
    row = jnp.zeros((1, LANES), jnp.float32)
    for j in range(ITERS + 1):
        for i in range(j + 1):
            for part in range(2):
                row = jnp.where(lane == part * 64 + 8 * j + i, columns[j][part][i : i + 1], row)
    msg_ref[...] = jnp.broadcast_to(row, msg_ref.shape)


def finish_kernel(count, got_ref, *refs):
    u_refs, z_refs = refs[: ITERS + 1], refs[ITERS + 1 : 2 * ITERS + 1]
    adj_ref, res_ref, flag_ref = refs[2 * ITERS + 1 :]
    lane = lax.broadcasted_iota(jnp.int32, (8, LANES), 1)
    rows = [got_ref[8 * k : 8 * k + 8, :] for k in range(count // 8)]
    pairs = [(jnp.where(lane < 64, row, 0.0), pltpu.roll(jnp.where(lane < 64, 0.0, row), 64, 1)) for row in rows]
    while len(pairs) > 1:
        pairs = [dd_add(pairs[k], pairs[k + 1]) for k in range(0, len(pairs), 2)]
    total = pairs[0]
    for shift in (4, 2, 1):
        total = dd_add(total, tuple(pltpu.roll(v, shift, 0) for v in total))

    def entry(i, j):
        i, j = min(i, j), max(i, j)
        at = 8 * j + i
        return tuple(jnp.broadcast_to(v[0:1, at : at + 1], (1, LANES)) for v in total)

    n = ITERS
    mat = [[entry(i + 1, j + 1) if j >= i else None for j in range(n)] for i in range(n)]
    vec = [entry(0, i + 1) for i in range(n)]
    norms = [mat[i][i][0] for i in range(n)]
    first = entry(0, 0)
    ok = (first[0] > 1e-20) & (first[0] < 1e30)
    left = first
    scaled = [None] * n
    factor = [[None] * n for _ in range(n)]
    for k in range(n):
        pivot = mat[k][k]
        ok = ok & (norms[k] > 1e-20) & (norms[k] < 1e30) & (pivot[0] > 1e-9 * norms[k])
        scaled[k] = dd_div(vec[k], pivot)
        left = dd_add(left, dd_neg(dd_mul(vec[k], scaled[k])))
        for j in range(k + 1, n):
            factor[k][j] = dd_div(mat[k][j], pivot)
        for i in range(k + 1, n):
            for j in range(i, n):
                mat[i][j] = dd_add(mat[i][j], dd_neg(dd_mul(factor[k][i], mat[k][j])))
            vec[i] = dd_add(vec[i], dd_neg(dd_mul(factor[k][i], vec[k])))
    coef = [None] * n
    for k in reversed(range(n)):
        value = scaled[k]
        for j in range(k + 1, n):
            value = dd_add(value, dd_neg(dd_mul(factor[k][j], coef[j])))
        coef[k] = value
    reach = jnp.zeros((1, LANES), jnp.float32)
    for k in range(n):
        reach = reach + jnp.abs(coef[k][0]) * jnp.sqrt(norms[k])
    ok = ok & (reach * reach < 1e7 * left[0])
    flag_ref[0] = jnp.min(jnp.where(ok, 1, 0))
    cells = adj_ref.shape[1]
    weight = [jnp.broadcast_to(coef[k][0][:, :1], (8, cells)) for k in range(n)]
    adj = weight[0] * z_refs[0][...]
    res = u_refs[0][...] - weight[0] * u_refs[1][...]
    for k in range(1, n):
        adj = adj + weight[k] * z_refs[k][...]
        res = res - weight[k] * u_refs[k + 1][...]
    adj_ref[...] = adj[:F]
    res_ref[...] = res[:F]


def shape(*dims):
    return jax.ShapeDtypeStruct(dims, jnp.float32)


def call(kernel, out, *args, name):
    return pl.pallas_call(
        kernel,
        out_shape=out,
        name=name,
        in_specs=[pl.BlockSpec(memory_space=pltpu.VMEM)] * len(args),
        out_specs=jax.tree.map(
            lambda o: pl.BlockSpec(memory_space=pltpu.SMEM if o.dtype == jnp.int32 else pltpu.VMEM), out
        ),
        compiler_params=pltpu.CompilerParams(vmem_limit_bytes=24 * 2**20),
    )(*args)


def per_device(rhs, diag_blocks, lower_blocks, upper_blocks, precond, coupling, send_cells, recv_cells, halo_len):
    fields, cells = rhs.shape
    peers = send_cells.shape[1]
    count = peers * lax.axis_size("grp")
    face = (precond, coupling, send_cells, halo_len)
    vector = shape(8, cells)
    message = shape(peers * 8, LANES)
    u, z, msg = call(first_kernel, (vector, vector, message), rhs, *face, name="first")
    us, zs, grams = [u], [z], []
    for col in range(ITERS):
        got = lax.all_to_all(msg.reshape(peers, 8, LANES), "blk", 0, 0, tiled=True)
        y, gram = call(
            functools.partial(local_kernel, col + 1),
            (vector, shape(2, 8, LANES)),
            zs[col], diag_blocks, lower_blocks, upper_blocks, *us,
            name="local",
        )
        grams.append(gram)
        got = got.reshape(peers * 8, LANES)
        if col < ITERS - 1:
            u, z, msg = call(step_kernel, (vector, vector, message), got, recv_cells, y, *face, name="step")
            zs.append(z)
        else:
            u, msg = call(last_kernel, (vector, shape(count, LANES)), got, recv_cells, y, *us, *grams, name="last")
        us.append(u)
    got = lax.all_to_all(msg, BOTH, 0, 0, tiled=True)
    adjoint, residual, flag = call(
        functools.partial(finish_kernel, count),
        (shape(fields, cells), shape(fields, cells), jax.ShapeDtypeStruct((1,), jnp.int32)),
        got, *us, *zs,
        name="finish",
    )
    return lax.cond(
        flag[0] == 1,
        lambda *args: (adjoint, residual),
        arnoldi,
        rhs, diag_blocks, lower_blocks, upper_blocks, precond, coupling, send_cells, recv_cells, halo_len,
    )


def solution(mesh):
    return jax.shard_map(
        per_device,
        mesh=mesh,
        in_specs=(
            P(None, BOTH),
            P(None, None, BOTH),
            P(None, None, BOTH),
            P(None, None, BOTH),
            P(None, None, BOTH),
            P(BOTH, None, None, None, None),
            P(BOTH, None, None),
            P(BOTH, None, None),
            P(BOTH, None),
        ),
        out_specs=(P(None, BOTH), P(None, BOTH)),
        check_vma=False,
    )
```

time: 1180 us -> 87.9 us (0.07); the launches traced: 1160 us -> 87.5 us
  blocking collectives: 679 us -> 0 us
  other arithmetic: 234 us -> 0 us
  local copies, waits for them, and re-layouts: 211 us -> 0.05 us
  waiting for transfers between devices: 0.02 us -> 40.1 us
  Pallas kernels: 0 us -> 14.2 us
    psum x9 -> x0, blocking collectives: 679 us -> none  [the longest x4 303 us: per_device(): proj = lax.psum(local_proj, ('blk', 'grp'))]
    scatter-add x5 -> x0, other arithmetic: 114 us -> none  [operate(): return local.at[:, recv_flat].add(term.reshape(fields, -1))]
    slice x39 -> x0, local copies, waits for them, and re-layouts: 77.4 us -> none  [the longest x30 71.8 us: mixing(): total = blocks[:, 0] * field[0][None]]
    gather x5 -> x0, local copies, waits for them, and re-layouts: 70.4 us -> none  [operate(): outgoing = jnp.take(field, send_flat, axis=1).reshape(fields, peers, width)]
    add x16 -> x0, other arithmetic: 59.2 us -> none  [the longest x5 41.4 us: operate(): mixing(diag_blocks, field) + mixing(lower_blocks, before)]
    all_to_all x6 -> x5, waiting for transfers between devices: 0.02 us -> 40.1 us  [the longest x4 27 us: per_device(): got = lax.all_to_all(msg.reshape(peers, 8, LANES), 'blk', 0, 0, tiled=True)]
    unnamed x150 -> x18, local copies, waits for them, and re-layouts: 28 us -> 0.05 us
    select_n x6 -> x0, other arithmetic: 23.7 us -> none  [the longest x5 23.7 us: operate(): outgoing = jnp.take(field, send_flat, axis=1).reshape(fields, peers, width)]
  transfers between devices with their start and end apart: 6 -> 5, of which waited for: 0 -> 5; matrix products, arithmetic and copies ran while one was open for 7% -> 0% of each run, Pallas kernels for 0% -> 4%
where the time goes in v1:
time: 87.9 us; the launch traced here: 87.5 us
  waiting for transfers between devices  40.1 us (46%)
  starting transfers between devices  31.2 us (35%)
  Pallas kernels  14.2 us (16%)
  between operations  1.7 us (2%)
    all_to_all x4, waiting for transfers between devices, per_device(): got = lax.all_to_all(msg.reshape(peers, 8, LANES), 'blk', 0, 0, tiled=True)  27 us
    all_to_all x4, starting transfers between devices, per_device(): got = lax.all_to_all(msg.reshape(peers, 8, LANES), 'blk', 0, 0, tiled=True)  20.3 us
    pallas_call x10, Pallas kernels, call(): pl.pallas_call(kernel, out_shape=out, name=name, in_specs=[pl.BlockSpec(m...  14.2 us
    all_to_all x1, waiting for transfers between devices, per_device(): got = lax.all_to_all(msg, BOTH, 0, 0, tiled=True)  13 us
    all_to_all x1, starting transfers between devices, per_device(): got = lax.all_to_all(msg, BOTH, 0, 0, tiled=True)  10.9 us
  transfers between devices with their start and end apart: 5, of which 5 were waited for; matrix products, arithmetic and copies ran while one was open for 0% of the time, Pallas kernels for 4%

profile of v1, /device:TPU:1, one launch (start us, length us, event | category | flops | bytes accessed | tf_op | source)
XLA Modules:
  0.0 87.5 jit_solution(1235593254398397697)
XLA Ops:
  0.6 0.0 copy-start.9
  0.6 0.0 copy-start.5
  0.7 0.0 copy-start.13
  0.7 0.0 copy-start.35
  0.7 0.0 copy-start.6
  0.7 0.0 copy-start.7
  0.7 0.0 copy-start.8
  0.7 0.0 copy-start.14
  0.7 2.5 %first.1 = (f32[8,1024]{1,0:T(8,128)S(1)}, f32[8,1024]{1,0:T(8,128)S(1)}, f32[256,128]{1,0:T(8,128)}) custom-call(f32[7,1024]{1,0:T(8,128)} %rhs_ref.1, f32[7,7,1024]{2,1,0:T(8,128)} %pre_ref.7, f32[1,7,7,32,128]{4,3,2,1,0:T(8,128)} %coup_ref.7, s32[1,32,128]{2,1,0:T(8,128)} %send_ref.7, s32[1,32]{1,0:T(1,128)} %halo_ref.7), custom_call_target="tpu_custom_call" | custom-call | tf_op jit(solution)/shard_map/first/pallas_call | solution.py:316
  3.3 8.6 %all-to-all-start.5 = ((f32[32,8,128]{2,1,0:T(8,128)}), f32[32,8,128]{2,1,0:T(8,128)S(1)}, u32[]{:S(2)}, u32[]{:S(2)}) async-start(f32[32,8,128]{2,1,0:T(8,128)} %bitcast.99), calls=%async_computation.5 | async-start | bytes 262144 | tf_op jit(solution)/shard_map/all_to_all | solution.py:338
  11.9 1.8 %local.4 = (f32[8,1024]{1,0:T(8,128)S(1)}, f32[2,8,128]{2,1,0:T(8,128)S(1)}) custom-call(f32[8,1024]{1,0:T(8,128)S(1)} %get-tuple-element.156.z_ref.refs_5_, f32[7,7,1024]{2,1,0:T(8,128)} %diag_ref.7, f32[7,7,1024]{2,1,0:T(8,128)} %low_ref.7, f32[7,7,1024]{2,1,0:T(8,128)} %up_ref.7, f32[8,1024]{1,0:T(8,128)S(1)} %get-tuple-element.157.refs_0_), custom_call_target="tpu_custom_call" | custom-call | tf_op jit(solution)/shard_map/local/pallas_call | solution.py:316
  13.6 5.9 %all-to-all-done.5 = f32[32,8,128]{2,1,0:T(8,128)S(1)} async-done(((f32[32,8,128]{2,1,0:T(8,128)}), f32[32,8,128]{2,1,0:T(8,128)S(1)}, u32[]{:S(2)}, u32[]{:S(2)}) %all-to-all-start.5) | async-done | bytes 131104 | tf_op jit(solution)/shard_map/all_to_all | solution.py:338
  19.5 0.0 copy-done.9
  19.5 0.0 copy-done.5
  19.5 1.6 %step.3 = (f32[8,1024]{1,0:T(8,128)S(1)}, f32[8,1024]{1,0:T(8,128)S(1)}, f32[256,128]{1,0:T(8,128)}) custom-call(f32[256,128]{1,0:T(8,128)S(1)} %bitcast.569, s32[1,32,128]{2,1,0:T(8,128)S(1)} %copy-done.14, f32[8,1024]{1,0:T(8,128)S(1)} %get-tuple-element.158.y_ref, f32[7,7,1024]{2,1,0:T(8,128)S(1)} %copy-done.9, f32[1,7,7,32,128]{4,3,2,1,0:T(8,128)S(1)} %copy-done.5, ...), custom_call_target="tpu_custom_call" | custom-call | tf_op jit(solution)/shard_map/step/pallas_call | solution.py:316
  21.1 3.9 %all-to-all-start.6 = ((f32[32,8,128]{2,1,0:T(8,128)}), f32[32,8,128]{2,1,0:T(8,128)S(1)}, u32[]{:S(2)}, u32[]{:S(2)}) async-start(f32[32,8,128]{2,1,0:T(8,128)} %bitcast.101), calls=%async_computation.6 | async-start | bytes 262144 | tf_op jit(solution)/shard_map/all_to_all | solution.py:338
  25.1 0.6 local.5
  25.7 7.1 %all-to-all-done.6 = f32[32,8,128]{2,1,0:T(8,128)S(1)} async-done(((f32[32,8,128]{2,1,0:T(8,128)}), f32[32,8,128]{2,1,0:T(8,128)S(1)}, u32[]{:S(2)}, u32[]{:S(2)}) %all-to-all-start.6) | async-done | bytes 131104 | tf_op jit(solution)/shard_map/all_to_all | solution.py:338
  32.8 1.6 %step.4 = (f32[8,1024]{1,0:T(8,128)S(1)}, f32[8,1024]{1,0:T(8,128)S(1)}, f32[256,128]{1,0:T(8,128)}) custom-call(f32[256,128]{1,0:T(8,128)S(1)} %bitcast.570, s32[1,32,128]{2,1,0:T(8,128)S(1)} %copy-done.14, f32[8,1024]{1,0:T(8,128)S(1)} %get-tuple-element.162.y_ref, f32[7,7,1024]{2,1,0:T(8,128)S(1)} %copy-done.9, f32[1,7,7,32,128]{4,3,2,1,0:T(8,128)S(1)} %copy-done.5, ...), custom_call_target="tpu_custom_call" | custom-call | tf_op jit(solution)/shard_map/step/pallas_call | solution.py:316
  34.4 3.9 %all-to-all-start.7 = ((f32[32,8,128]{2,1,0:T(8,128)}), f32[32,8,128]{2,1,0:T(8,128)S(1)}, u32[]{:S(2)}, u32[]{:S(2)}) async-start(f32[32,8,128]{2,1,0:T(8,128)} %bitcast.103), calls=%async_computation.7 | async-start | bytes 262144 | tf_op jit(solution)/shard_map/all_to_all | solution.py:338
  38.3 0.0 copy-start.17
  38.4 0.7 local.6
  39.0 7.1 %all-to-all-done.7 = f32[32,8,128]{2,1,0:T(8,128)S(1)} async-done(((f32[32,8,128]{2,1,0:T(8,128)}), f32[32,8,128]{2,1,0:T(8,128)S(1)}, u32[]{:S(2)}, u32[]{:S(2)}) %all-to-all-start.7) | async-done | bytes 131104 | tf_op jit(solution)/shard_map/all_to_all | solution.py:338
  46.1 1.6 %step.5 = (f32[8,1024]{1,0:T(8,128)S(1)}, f32[8,1024]{1,0:T(8,128)S(1)}, f32[256,128]{1,0:T(8,128)}) custom-call(f32[256,128]{1,0:T(8,128)S(1)} %bitcast.571, s32[1,32,128]{2,1,0:T(8,128)S(1)} %copy-done.14, f32[8,1024]{1,0:T(8,128)S(1)} %get-tuple-element.166.y_ref, f32[7,7,1024]{2,1,0:T(8,128)S(1)} %copy-done.9, f32[1,7,7,32,128]{4,3,2,1,0:T(8,128)S(1)} %copy-done.5, ...), custom_call_target="tpu_custom_call" | custom-call | tf_op jit(solution)/shard_map/step/pallas_call | solution.py:316
  47.7 3.9 %all-to-all-start.8 = ((f32[32,8,128]{2,1,0:T(8,128)}), f32[32,8,128]{2,1,0:T(8,128)S(1)}, u32[]{:S(2)}, u32[]{:S(2)}) async-start(f32[32,8,128]{2,1,0:T(8,128)} %bitcast.105), calls=%async_computation.8 | async-start | bytes 262144 | tf_op jit(solution)/shard_map/all_to_all | solution.py:338
  51.6 0.7 local.7
  52.3 7.1 %all-to-all-done.8 = f32[32,8,128]{2,1,0:T(8,128)S(1)} async-done(((f32[32,8,128]{2,1,0:T(8,128)}), f32[32,8,128]{2,1,0:T(8,128)S(1)}, u32[]{:S(2)}, u32[]{:S(2)}) %all-to-all-start.8) | async-done | bytes 131104 | tf_op jit(solution)/shard_map/all_to_all | solution.py:338
  59.4 1.9 %last.1 = (f32[8,1024]{1,0:T(8,128)S(1)}, f32[256,128]{1,0:T(8,128)}) custom-call(f32[256,128]{1,0:T(8,128)S(1)} %bitcast.573, s32[1,32,128]{2,1,0:T(8,128)S(1)} %copy-done.14, f32[8,1024]{1,0:T(8,128)S(1)} %get-tuple-element.170.y_ref, f32[8,1024]{1,0:T(8,128)S(1)} %get-tuple-element.157.refs_0_, f32[8,1024]{1,0:T(8,128)S(1)} %get-tuple-element.161.refs_1_, ...), custom_call_target="tpu_custom_call" | custom-call | tf_op jit(solution)/shard_map/last/pallas_call | solution.py:316
  61.3 10.9 %all-to-all-start.9 = ((f32[256,1,128]{2,1,0:T(1,128)}), f32[256,1,128]{2,1,0:T(1,128)S(1)}, u32[]{:S(2)}, u32[]{:S(2)}) async-start(f32[256,1,128]{2,1,0:T(1,128)} %bitcast.108), calls=%async_computation.9 | async-start | bytes 262144 | tf_op jit(solution)/shard_map/all_to_all | solution.py:353
  72.2 13.0 %all-to-all-done.9 = f32[256,1,128]{2,1,0:T(1,128)S(1)} async-done(((f32[256,1,128]{2,1,0:T(1,128)}), f32[256,1,128]{2,1,0:T(1,128)S(1)}, u32[]{:S(2)}, u32[]{:S(2)}) %all-to-all-start.9) | async-done | bytes 131104 | tf_op jit(solution)/shard_map/all_to_all | solution.py:353
  85.2 1.1 %finish.1 = (f32[7,1024]{1,0:T(8,128)}, f32[7,1024]{1,0:T(8,128)}, s32[1]{0:T(128)}) custom-call(f32[256,128]{1,0:T(8,128)S(1)} %bitcast.572, f32[8,1024]{1,0:T(8,128)S(1)} %get-tuple-element.157.refs_0_, f32[8,1024]{1,0:T(8,128)S(1)} %get-tuple-element.161.refs_1_, f32[8,1024]{1,0:T(8,128)S(1)} %get-tuple-element.165.refs_2_, ...), custom_call_target="tpu_custom_call" | custom-call | tf_op jit(solution)/shard_map/finish/pallas_call | solution.py:316
  87.1 0.2 conditional.1
  (7 shorter events, 0.0 us)
Async XLA Ops:
  0.6 18.9 %copy-start.9 = (f32[7,7,1024]{2,1,0:T(8,128)S(1)}, f32[7,7,1024]{2,1,0:T(8,128)}, u32[]{:S(2)}) copy-start(f32[7,7,1024]{2,1,0:T(8,128)} %pre_ref.7) | copy-start | bytes 602116
  0.6 18.9 %copy-start.5 = (f32[1,7,7,32,128]{4,3,2,1,0:T(8,128)S(1)}, f32[1,7,7,32,128]{4,3,2,1,0:T(8,128)}, u32[]{:S(2)}) copy-start(f32[1,7,7,32,128]{4,3,2,1,0:T(8,128)} %coup_ref.7) | copy-start | bytes 2408452
  0.7 18.8 %copy-start.13 = (s32[1,32,128]{2,1,0:T(8,128)S(1)}, s32[1,32,128]{2,1,0:T(8,128)}, u32[]{:S(2)}) copy-start(s32[1,32,128]{2,1,0:T(8,128)} %send_ref.7) | copy-start | bytes 49156
  0.7 18.8 %copy-start.35 = (s32[1,32]{1,0:T(1,128)S(1)}, s32[1,32]{1,0:T(1,128)}, u32[]{:S(2)}) copy-start(s32[1,32]{1,0:T(1,128)} %halo_ref.7) | copy-start | bytes 388
  0.7 24.4 %copy-start.6 = (f32[7,7,1024]{2,1,0:T(8,128)S(1)}, f32[7,7,1024]{2,1,0:T(8,128)}, u32[]{:S(2)}) copy-start(f32[7,7,1024]{2,1,0:T(8,128)} %diag_ref.7) | copy-start | bytes 602116
  0.7 24.4 %copy-start.7 = (f32[7,7,1024]{2,1,0:T(8,128)S(1)}, f32[7,7,1024]{2,1,0:T(8,128)}, u32[]{:S(2)}) copy-start(f32[7,7,1024]{2,1,0:T(8,128)} %low_ref.7) | copy-start | bytes 602116
  0.7 24.4 %copy-start.8 = (f32[7,7,1024]{2,1,0:T(8,128)S(1)}, f32[7,7,1024]{2,1,0:T(8,128)}, u32[]{:S(2)}) copy-start(f32[7,7,1024]{2,1,0:T(8,128)} %up_ref.7) | copy-start | bytes 602116
  0.7 18.8 %copy-start.14 = (s32[1,32,128]{2,1,0:T(8,128)S(1)}, s32[1,32,128]{2,1,0:T(8,128)}, u32[]{:S(2)}) copy-start(s32[1,32,128]{2,1,0:T(8,128)} %cells_ref.7) | copy-start | bytes 49156
  3.3 16.2 %all-to-all-start.5 = ((f32[32,8,128]{2,1,0:T(8,128)}), f32[32,8,128]{2,1,0:T(8,128)S(1)}, u32[]{:S(2)}, u32[]{:S(2)}) async-start(f32[32,8,128]{2,1,0:T(8,128)} %bitcast.99), calls=%async_computation.5 | async-start | bytes 262144 | tf_op jit(solution)/shard_map/all_to_all | solution.py:338
  21.1 11.7 %all-to-all-start.6 = ((f32[32,8,128]{2,1,0:T(8,128)}), f32[32,8,128]{2,1,0:T(8,128)S(1)}, u32[]{:S(2)}, u32[]{:S(2)}) async-start(f32[32,8,128]{2,1,0:T(8,128)} %bitcast.101), calls=%async_computation.6 | async-start | bytes 262144 | tf_op jit(solution)/shard_map/all_to_all | solution.py:338
  34.4 11.7 %all-to-all-start.7 = ((f32[32,8,128]{2,1,0:T(8,128)}), f32[32,8,128]{2,1,0:T(8,128)S(1)}, u32[]{:S(2)}, u32[]{:S(2)}) async-start(f32[32,8,128]{2,1,0:T(8,128)} %bitcast.103), calls=%async_computation.7 | async-start | bytes 262144 | tf_op jit(solution)/shard_map/all_to_all | solution.py:338
  38.3 48.7 %copy-start.17 = (f32[7,1024]{1,0:T(8,128)S(1)}, f32[7,1024]{1,0:T(8,128)}, u32[]{:S(2)}) copy-start(f32[7,1024]{1,0:T(8,128)} %rhs_ref.1) | copy-start | bytes 86020
  47.7 11.7 %all-to-all-start.8 = ((f32[32,8,128]{2,1,0:T(8,128)}), f32[32,8,128]{2,1,0:T(8,128)S(1)}, u32[]{:S(2)}, u32[]{:S(2)}) async-start(f32[32,8,128]{2,1,0:T(8,128)} %bitcast.105), calls=%async_computation.8 | async-start | bytes 262144 | tf_op jit(solution)/shard_map/all_to_all | solution.py:338
  61.3 23.9 %all-to-all-start.9 = ((f32[256,1,128]{2,1,0:T(1,128)}), f32[256,1,128]{2,1,0:T(1,128)S(1)}, u32[]{:S(2)}, u32[]{:S(2)}) async-start(f32[256,1,128]{2,1,0:T(1,128)} %bitcast.108), calls=%async_computation.9 | async-start | bytes 262144 | tf_op jit(solution)/shard_map/all_to_all | solution.py:353

commit v2 on v1

--- a/solution.py
+++ b/solution.py
@@ -100,10 +100,10 @@
     return -a[0], -a[1]
 
 
-def dd_div(a, b):
-    q = a[0] / b[0]
+def dd_over(a, b, inverse):
+    q = a[0] * inverse
     rest = dd_add(a, dd_neg(dd_mul(b, (q, jnp.zeros_like(q)))))
-    return quick_sum(q, rest[0] / b[0])
+    return quick_sum(q, rest[0] * inverse)
 
 
 def row_sums(parts):
@@ -115,35 +115,41 @@
     return row_sums([pre_ref[i] * u[:F] for i in range(F)])
 
 
-def write_message(z, coup_ref, send_ref, halo_ref, msg_ref):
+def gather(z, send_ref):
     cells = z.shape[1]
     tiles = cells // LANES
-    peers = send_ref.shape[1]
     source = [
         [jnp.broadcast_to(z[f : f + 1, t * LANES : (t + 1) * LANES], (8, LANES)) for t in range(tiles)]
         for f in range(F)
     ]
+    taken = []
+    for q in range(send_ref.shape[1] // 8):
+        cell = send_ref[0, q * 8 : (q + 1) * 8, :]
+        low = cell & (LANES - 1)
+        high = cell >> 7
+        taken.append([])
+        for f in range(F):
+            got = jnp.take_along_axis(source[f][0], low, axis=1, mode="promise_in_bounds")
+            for t in range(1, tiles):
+                other = jnp.take_along_axis(source[f][t], low, axis=1, mode="promise_in_bounds")
+                got = jnp.where(high == t, other, got)
+            taken[q].append(got)
+    return taken
+
+
+def mix(taken, coup_ref, halo_ref, msg_ref):
+    peers = halo_ref.shape[1]
     lanes = lax.broadcasted_iota(jnp.int32, (8, LANES), 1)
     rows = lax.broadcasted_iota(jnp.int32, (8, peers), 0)
     cols = lax.broadcasted_iota(jnp.int32, (8, peers), 1)
     lens = jnp.broadcast_to(halo_ref[...], (8, peers))
     for q in range(peers // 8):
-        cell = send_ref[0, q * 8 : (q + 1) * 8, :]
-        low = cell & (LANES - 1)
-        high = cell >> 7
         size = jnp.sum(jnp.where(cols == rows + q * 8, lens, 0), axis=1, keepdims=True)
         live = lanes < size
-        taken = []
-        for f in range(F):
-            got = jnp.take_along_axis(source[f][0], low, axis=1, mode="promise_in_bounds")
-            for t in range(1, tiles):
-                other = jnp.take_along_axis(source[f][t], low, axis=1, mode="promise_in_bounds")
-                got = jnp.where(high == t, other, got)
-            taken.append(got)
         for i in range(F):
-            total = coup_ref[0, i, 0, q * 8 : (q + 1) * 8, :] * taken[0]
+            total = coup_ref[0, i, 0, q * 8 : (q + 1) * 8, :] * taken[q][0]
             for j in range(1, F):
-                total = total + coup_ref[0, i, j, q * 8 : (q + 1) * 8, :] * taken[j]
+                total = total + coup_ref[0, i, j, q * 8 : (q + 1) * 8, :] * taken[q][j]
             msg_ref[pl.ds(q * 64 + i, 8, stride=8), :] = jnp.where(live, total, 0.0)
         msg_ref[pl.ds(q * 64 + F, 8, stride=8), :] = jnp.zeros((8, LANES), jnp.float32)
 
@@ -180,6 +186,15 @@
     return jnp.concatenate(out, axis=1)
 
 
+def local_part(z, diag_ref, low_ref, up_ref):
+    cells = z.shape[1]
+    col = lax.broadcasted_iota(jnp.int32, z.shape, 1)
+    before = jnp.where(col == 0, 0.0, pltpu.roll(z, 1, 1))[:F]
+    after = jnp.where(col == cells - 1, 0.0, pltpu.roll(z, cells - 1, 1))[:F]
+    z = z[:F]
+    return row_sums([diag_ref[i] * z + low_ref[i] * before + up_ref[i] * after for i in range(F)])
+
+
 def products(us, last):
     cells = last.shape[1]
     tiles = [slice(t * LANES, (t + 1) * LANES) for t in range(cells // LANES)]
@@ -199,39 +214,53 @@
             total = dd_add(total, tuple(pltpu.roll(v, shift, 0) for v in total))
         hi = jnp.where(rows == i, total[0], hi)
         lo = jnp.where(rows == i, total[1], lo)
-    total = (hi, lo)
-    for shift in (64, 32, 16, 8, 4, 2, 1):
-        total = dd_add(total, tuple(pltpu.roll(v, shift, 1) for v in total))
-    return total
-
-
-def first_kernel(rhs_ref, pre_ref, coup_ref, send_ref, halo_ref, u_ref, z_ref, msg_ref):
+    return hi, lo
+
+
+def lane_sum(hi, lo):
+    top = jnp.max(jnp.abs(hi), axis=1, keepdims=True) * 8192.0
+    coarse = (hi + top) - top
+    fine = (hi - coarse) + lo
+    return quick_sum(jnp.sum(coarse, axis=1, keepdims=True), jnp.sum(fine, axis=1, keepdims=True))
+
+
+def first_kernel(
+    rhs_hbm, pre_hbm, coup_hbm, send_hbm, halo_hbm, diag_hbm, low_hbm, up_hbm, cells_hbm,
+    u_ref, z_ref, msg_ref, y_ref, gram_ref, pre_ref, coup_ref, send_ref, halo_ref, diag_ref, low_ref, up_ref, cells_ref,
+    rhs_ref, sems,
+):
+    whole = [(rhs_hbm, rhs_ref), (send_hbm, send_ref), (halo_hbm, halo_ref)]
+    rows = [(pre_hbm.at[i], pre_ref.at[i]) for i in range(F)]
+    faces = [(coup_hbm.at[0, i], coup_ref.at[0, i]) for i in range(F)]
+    blocks = [(diag_hbm, diag_ref), (low_hbm, low_ref), (up_hbm, up_ref), (cells_hbm, cells_ref)]
+    copies = [pltpu.make_async_copy(*pair, sems.at[k]) for k, pair in enumerate(whole + rows + faces + blocks)]
+    for copy in copies:
+        copy.start()
+    for copy in copies[: len(whole) + F]:
+        copy.wait()
     u = jnp.concatenate([rhs_ref[...], jnp.zeros((1, rhs_ref.shape[1]), jnp.float32)], axis=0)
     z = precondition(pre_ref, u)
     u_ref[...] = u
     z_ref[...] = z
-    write_message(z, coup_ref, send_ref, halo_ref, msg_ref)
-
-
-def local_kernel(count, z_ref, diag_ref, low_ref, up_ref, *refs):
-    u_refs, (y_ref, gram_ref) = refs[:count], refs[count:]
-    z = z_ref[...]
-    cells = z.shape[1]
-    col = lax.broadcasted_iota(jnp.int32, z.shape, 1)
-    before = jnp.where(col == 0, 0.0, pltpu.roll(z, 1, 1))[:F]
-    after = jnp.where(col == cells - 1, 0.0, pltpu.roll(z, cells - 1, 1))[:F]
-    z = z[:F]
-    y_ref[...] = row_sums([diag_ref[i] * z + low_ref[i] * before + up_ref[i] * after for i in range(F)])
-    us = [ref[...] for ref in u_refs]
-    gram_ref[0], gram_ref[1] = products(us, us[-1])
-
-
-def step_kernel(recv_ref, cells_ref, y_ref, pre_ref, coup_ref, send_ref, halo_ref, u_ref, z_ref, msg_ref):
+    gram_ref[0], gram_ref[1] = products([u], u)
+    taken = gather(z, send_ref)
+    for copy in copies[len(whole) + F : len(whole) + 2 * F]:
+        copy.wait()
+    mix(taken, coup_ref, halo_ref, msg_ref)
+    for copy in copies[len(whole) + 2 * F :]:
+        copy.wait()
+    y_ref[...] = local_part(z, diag_ref, low_ref, up_ref)
+
+
+def step_kernel(col, recv_ref, cells_ref, y_ref, pre_ref, coup_ref, send_ref, halo_ref, diag_ref, low_ref, up_ref, *refs):
+    u_refs, (u_ref, z_ref, msg_ref, next_ref, gram_ref) = refs[:col], refs[col:]
     u = y_ref[...] + scatter(recv_ref, cells_ref, y_ref.shape[1] // LANES)
     z = precondition(pre_ref, u)
     u_ref[...] = u
     z_ref[...] = z
-    write_message(z, coup_ref, send_ref, halo_ref, msg_ref)
+    mix(gather(z, send_ref), coup_ref, halo_ref, msg_ref)
+    next_ref[...] = local_part(z, diag_ref, low_ref, up_ref)
+    gram_ref[0], gram_ref[1] = products([ref[...] for ref in u_refs] + [u], u)
 
 
 def last_kernel(recv_ref, cells_ref, y_ref, *refs):
@@ -240,13 +269,14 @@
     u_ref[...] = u
     columns = [(ref[0], ref[1]) for ref in gram_refs]
     columns.append(products([ref[...] for ref in u_refs] + [u], u))
-    lane = lax.broadcasted_iota(jnp.int32, (1, LANES), 1)
-    row = jnp.zeros((1, LANES), jnp.float32)
+    lane = lax.broadcasted_iota(jnp.int32, (8, LANES), 1)
+    row = lax.broadcasted_iota(jnp.int32, (8, LANES), 0)
+    placed = jnp.zeros((8, LANES), jnp.float32)
     for j in range(ITERS + 1):
-        for i in range(j + 1):
-            for part in range(2):
-                row = jnp.where(lane == part * 64 + 8 * j + i, columns[j][part][i : i + 1], row)
-    msg_ref[...] = jnp.broadcast_to(row, msg_ref.shape)
+        for part, total in enumerate(lane_sum(*columns[j])):
+            placed = jnp.where(lane == row + (part * 64 + 8 * j), total, placed)
+    placed = jnp.sum(placed, axis=0, keepdims=True)
+    msg_ref[...] = jnp.broadcast_to(placed, msg_ref.shape)
 
 
 def finish_kernel(count, got_ref, *refs):
@@ -254,12 +284,13 @@
     adj_ref, res_ref, flag_ref = refs[2 * ITERS + 1 :]
     lane = lax.broadcasted_iota(jnp.int32, (8, LANES), 1)
     rows = [got_ref[8 * k : 8 * k + 8, :] for k in range(count // 8)]
-    pairs = [(jnp.where(lane < 64, row, 0.0), pltpu.roll(jnp.where(lane < 64, 0.0, row), 64, 1)) for row in rows]
+    pairs = [two_sum(rows[k], rows[k + 1]) for k in range(0, len(rows), 2)]
     while len(pairs) > 1:
         pairs = [dd_add(pairs[k], pairs[k + 1]) for k in range(0, len(pairs), 2)]
     total = pairs[0]
     for shift in (4, 2, 1):
         total = dd_add(total, tuple(pltpu.roll(v, shift, 0) for v in total))
+    total = dd_add(total, tuple(pltpu.roll(v, 64, 1) for v in total))
 
     def entry(i, j):
         i, j = min(i, j), max(i, j)
@@ -278,10 +309,11 @@
     for k in range(n):
         pivot = mat[k][k]
         ok = ok & (norms[k] > 1e-20) & (norms[k] < 1e30) & (pivot[0] > 1e-9 * norms[k])
-        scaled[k] = dd_div(vec[k], pivot)
+        inverse = 1.0 / pivot[0]
+        scaled[k] = dd_over(vec[k], pivot, inverse)
         left = dd_add(left, dd_neg(dd_mul(vec[k], scaled[k])))
         for j in range(k + 1, n):
-            factor[k][j] = dd_div(mat[k][j], pivot)
+            factor[k][j] = dd_over(mat[k][j], pivot, inverse)
         for i in range(k + 1, n):
             for j in range(i, n):
                 mat[i][j] = dd_add(mat[i][j], dd_neg(dd_mul(factor[k][i], mat[k][j])))
@@ -312,15 +344,16 @@
     return jax.ShapeDtypeStruct(dims, jnp.float32)
 
 
-def call(kernel, out, *args, name):
+def call(kernel, out, *args, name, space=pltpu.VMEM, scratch=()):
     return pl.pallas_call(
         kernel,
         out_shape=out,
         name=name,
-        in_specs=[pl.BlockSpec(memory_space=pltpu.VMEM)] * len(args),
-        out_specs=jax.tree.map(
-            lambda o: pl.BlockSpec(memory_space=pltpu.SMEM if o.dtype == jnp.int32 else pltpu.VMEM), out
+        in_specs=[pl.BlockSpec(memory_space=space)] * len(args),
+        out_specs=tuple(
+            pl.BlockSpec(memory_space=pltpu.SMEM if o.shape == (1,) else pltpu.VMEM) for o in out
         ),
+        scratch_shapes=scratch,
         compiler_params=pltpu.CompilerParams(vmem_limit_bytes=24 * 2**20),
     )(*args)
 
@@ -329,24 +362,33 @@
     fields, cells = rhs.shape
     peers = send_cells.shape[1]
     count = peers * lax.axis_size("grp")
-    face = (precond, coupling, send_cells, halo_len)
     vector = shape(8, cells)
     message = shape(peers * 8, LANES)
-    u, z, msg = call(first_kernel, (vector, vector, message), rhs, *face, name="first")
-    us, zs, grams = [u], [z], []
+    args = (rhs, diag_blocks, lower_blocks, upper_blocks, precond, coupling, send_cells, recv_cells, halo_len)
+    blocks = (diag_blocks, lower_blocks, upper_blocks)
+    gram_shape = shape(2, 8, LANES)
+    inputs = (precond, coupling, send_cells, halo_len, *blocks, recv_cells)
+    u, z, msg, y, gram, *kept = call(
+        first_kernel,
+        (vector, vector, message, vector, gram_shape, *(jax.ShapeDtypeStruct(a.shape, a.dtype) for a in inputs)),
+        rhs, *inputs,
+        name="first",
+        space=pltpu.HBM,
+        scratch=(pltpu.VMEM(rhs.shape, jnp.float32), pltpu.SemaphoreType.DMA((2 * fields + 7,))),
+    )
+    face, blocks, recv_cells = kept[:4], kept[4:7], kept[7]
+    us, zs, grams = [u], [z], [gram]
     for col in range(ITERS):
-        got = lax.all_to_all(msg.reshape(peers, 8, LANES), "blk", 0, 0, tiled=True)
-        y, gram = call(
-            functools.partial(local_kernel, col + 1),
-            (vector, shape(2, 8, LANES)),
-            zs[col], diag_blocks, lower_blocks, upper_blocks, *us,
-            name="local",
-        )
-        grams.append(gram)
-        got = got.reshape(peers * 8, LANES)
+        got = lax.all_to_all(msg.reshape(peers, 8, LANES), "blk", 0, 0, tiled=True).reshape(peers * 8, LANES)
         if col < ITERS - 1:
-            u, z, msg = call(step_kernel, (vector, vector, message), got, recv_cells, y, *face, name="step")
+            u, z, msg, y, gram = call(
+                functools.partial(step_kernel, col + 1),
+                (vector, vector, message, vector, gram_shape),
+                got, recv_cells, y, *face, *blocks, *us,
+                name="step",
+            )
             zs.append(z)
+            grams.append(gram)
         else:
             u, msg = call(last_kernel, (vector, shape(count, LANES)), got, recv_cells, y, *us, *grams, name="last")
         us.append(u)
@@ -357,12 +399,8 @@
         got, *us, *zs,
         name="finish",
     )
-    return lax.cond(
-        flag[0] == 1,
-        lambda *args: (adjoint, residual),
-        arnoldi,
-        rhs, diag_blocks, lower_blocks, upper_blocks, precond, coupling, send_cells, recv_cells, halo_len,
-    )
+    args, adjoint, residual, flag = lax.optimization_barrier((args, adjoint, residual, flag))
+    return lax.switch(flag[0], [lambda *_: arnoldi(*args), lambda *outs: outs], adjoint, residual)
 
 
 def solution(mesh):

time: 87.9 us -> 83.2 us (0.947)
  blocking collectives: 0 us -> 73.7 us
  waiting for transfers between devices: 40.1 us -> 0 us
  starting transfers between devices: 31.2 us -> 0 us
  Pallas kernels: 14.2 us -> 7.2 us
    all_to_all x0 -> x5, blocking collectives: none -> 73.7 us  [the longest x4 50 us: per_device(): lax.all_to_all(msg.reshape(peers, 8, LANES), 'blk', 0, 0, tiled=True)]
    all_to_all x5 -> x0, waiting for transfers between devices: 40.1 us -> none  [the longest x4 27 us: per_device(): got = lax.all_to_all(msg.reshape(peers, 8, LANES), 'blk', 0, 0, tiled=True)]
    all_to_all x5 -> x0, starting transfers between devices: 31.2 us -> none  [the longest x4 20.3 us: per_device(): got = lax.all_to_all(msg.reshape(peers, 8, LANES), 'blk', 0, 0, tiled=True)]
    pallas_call x10 -> x6, Pallas kernels: 14.2 us -> 7.2 us  [call(): pl.pallas_call(kernel, out_shape=out, name=name, in_specs=[pl.BlockSpec(m...]
  transfers between devices with their start and end apart: 5 -> 0, of which waited for: 5 -> 0; matrix products, arithmetic and copies ran while one was open for 0% -> 0% of each run, Pallas kernels for 4% -> 0%
where the time goes in v2:
time: 83.2 us; the launch traced here: 82.9 us
  blocking collectives  73.7 us (89%)
  Pallas kernels  7.2 us (9%)
  between operations  1.68 us (2%)
    all_to_all x4, blocking collectives, per_device(): lax.all_to_all(msg.reshape(peers, 8, LANES), 'blk', 0, 0, tiled=True)  50 us
    all_to_all x1, blocking collectives, per_device(): got = lax.all_to_all(msg, BOTH, 0, 0, tiled=True)  23.8 us
    pallas_call x6, Pallas kernels, call(): pl.pallas_call(kernel, out_shape=out, name=name, in_specs=[pl.BlockSpec(m...  7.2 us

profile of v2, /device:TPU:1, one launch (start us, length us, event | category | flops | bytes accessed | tf_op | source)
XLA Modules:
  0.0 82.9 jit_solution(3891214336845718730)
XLA Ops:
  0.6 1.9 %first.1 = (f32[8,1024]{1,0:T(8,128)S(1)}, f32[8,1024]{1,0:T(8,128)S(1)}, f32[256,128]{1,0:T(8,128)S(1)}, f32[8,1024]{1,0:T(8,128)S(1)}, f32[2,8,128]{2,1,0:T(8,...) custom-call(f32[7,1024]{1,0:T(8,128)} %rhs_hbm.1, ...), custom_call_target="tpu_custom_call" | custom-call | tf_op jit(solution)/shard_map/first/pallas_call | solution.py:348
  2.6 16.0 %all_to_all.51 = f32[32,8,128]{2,1,0:T(8,128)S(1)} all-to-all(f32[32,8,128]{2,1,0:T(8,128)S(1)} %bitcast.575), channel_id=1, replica_groups=mesh['blk'=32,'grp'=8] {'blk'}, dimensions={0} | all-to-all | bytes 262144 | tf_op jit(solution)/shard_map/all_to_all | solution.py:382
  18.6 1.1 %step.3 = (f32[8,1024]{1,0:T(8,128)S(1)}, f32[8,1024]{1,0:T(8,128)S(1)}, f32[256,128]{1,0:T(8,128)S(1)}, f32[8,1024]{1,0:T(8,128)S(1)}, f32[2,8,128]{2,1,0:T(8,128)S(1)}) custom-call(f32[256,128]{1,0:T(8,128)S(1)} %bitcast.570, s32[1,32,128]{2,1,0:T(8,128)S(1)} %get-tuple-element.176.cells_ref, f32[8,1024]{1,0:T(8,128)S(1)} %get-tuple-element.177.y_ref, ...), custom_call_target="tpu_custom_call" | custom-call | tf_op jit(solution)/shard_map/step/pallas_call | solution.py:348
  19.7 11.3 %all_to_all.52 = f32[32,8,128]{2,1,0:T(8,128)S(1)} all-to-all(f32[32,8,128]{2,1,0:T(8,128)S(1)} %bitcast.577), channel_id=1, replica_groups=mesh['blk'=32,'grp'=8] {'blk'}, dimensions={0} | all-to-all | bytes 262144 | tf_op jit(solution)/shard_map/all_to_all | solution.py:382
  30.9 1.1 %step.4 = (f32[8,1024]{1,0:T(8,128)S(1)}, f32[8,1024]{1,0:T(8,128)S(1)}, f32[256,128]{1,0:T(8,128)S(1)}, f32[8,1024]{1,0:T(8,128)S(1)}, f32[2,8,128]{2,1,0:T(8,128)S(1)}) custom-call(f32[256,128]{1,0:T(8,128)S(1)} %bitcast.571, s32[1,32,128]{2,1,0:T(8,128)S(1)} %get-tuple-element.176.cells_ref, f32[8,1024]{1,0:T(8,128)S(1)} %get-tuple-element.187.y_ref, ...), custom_call_target="tpu_custom_call" | custom-call | tf_op jit(solution)/shard_map/step/pallas_call | solution.py:348
  32.0 0.0 copy-start.5
  32.0 0.0 copy-start.6
  32.0 0.0 copy-start.7
  32.1 0.0 copy-start.8
  32.1 0.0 copy-start.14
  32.1 0.0 copy-start.15
  32.1 0.0 copy-start.16
  32.1 0.0 copy-start.38
  32.1 11.4 %all_to_all.53 = f32[32,8,128]{2,1,0:T(8,128)S(1)} all-to-all(f32[32,8,128]{2,1,0:T(8,128)S(1)} %bitcast.578), channel_id=1, replica_groups=mesh['blk'=32,'grp'=8] {'blk'}, dimensions={0} | all-to-all | bytes 262144 | tf_op jit(solution)/shard_map/all_to_all | solution.py:382
  43.5 1.1 %step.5 = (f32[8,1024]{1,0:T(8,128)S(1)}, f32[8,1024]{1,0:T(8,128)S(1)}, f32[256,128]{1,0:T(8,128)S(1)}, f32[8,1024]{1,0:T(8,128)S(1)}, f32[2,8,128]{2,1,0:T(8,128)S(1)}) custom-call(f32[256,128]{1,0:T(8,128)S(1)} %bitcast.569, s32[1,32,128]{2,1,0:T(8,128)S(1)} %get-tuple-element.176.cells_ref, f32[8,1024]{1,0:T(8,128)S(1)} %get-tuple-element.190.y_ref, ...), custom_call_target="tpu_custom_call" | custom-call | tf_op jit(solution)/shard_map/step/pallas_call | solution.py:348
  44.6 11.3 %all_to_all.54 = f32[32,8,128]{2,1,0:T(8,128)S(1)} all-to-all(f32[32,8,128]{2,1,0:T(8,128)S(1)} %bitcast.574), channel_id=1, replica_groups=mesh['blk'=32,'grp'=8] {'blk'}, dimensions={0} | all-to-all | bytes 262144 | tf_op jit(solution)/shard_map/all_to_all | solution.py:382
  55.9 0.9 %last.1 = (f32[8,1024]{1,0:T(8,128)S(1)}, f32[256,128]{1,0:T(8,128)S(1)}) custom-call(f32[256,128]{1,0:T(8,128)S(1)} %bitcast.573, s32[1,32,128]{2,1,0:T(8,128)S(1)} %get-tuple-element.176.cells_ref, f32[8,1024]{1,0:T(8,128)S(1)} %get-tuple-element.193.y_ref, f32[8,1024]{1,0:T(8,128)S(1)} %get-tuple-element.185.refs_0_, ...), custom_call_target="tpu_custom_call" | custom-call | tf_op jit(solution)/shard_map/last/pallas_call | solution.py:348
  56.8 23.8 %all_to_all.55 = f32[256,1,128]{2,1,0:T(1,128)S(1)} all-to-all(f32[256,1,128]{2,1,0:T(1,128)S(1)} %bitcast.576), channel_id=1, replica_groups=mesh['blk'=32,'grp'=8] {'blk','grp'}, dimensions={0} | all-to-all | bytes 262144 | tf_op jit(solution)/shard_map/all_to_all | solution.py:395
  80.6 1.1 %finish.1 = (f32[7,1024]{1,0:T(8,128)}, f32[7,1024]{1,0:T(8,128)}, s32[1]{0:T(128)}) custom-call(f32[256,128]{1,0:T(8,128)S(1)} %bitcast.572, f32[8,1024]{1,0:T(8,128)S(1)} %get-tuple-element.185.refs_0_, f32[8,1024]{1,0:T(8,128)S(1)} %get-tuple-element.188.refs_1_, f32[8,1024]{1,0:T(8,128)S(1)} %get-tuple-element.191.refs_2_, ...), custom_call_target="tpu_custom_call" | custom-call | tf_op jit(solution)/shard_map/finish/pallas_call | solution.py:348
  82.4 0.0 copy-done.5
  82.4 0.0 copy-done.6
  82.4 0.0 copy-done.7
  82.4 0.0 copy-done.8
  82.4 0.0 copy-done.14
  82.4 0.0 copy-done.15
  82.5 0.0 copy-done.16
  82.5 0.0 copy-done.38
  82.5 0.2 conditional.1
Async XLA Ops:
  32.0 50.4 %copy-start.5 = (f32[1,7,7,32,128]{4,3,2,1,0:T(8,128)S(1)}, f32[1,7,7,32,128]{4,3,2,1,0:T(8,128)}, u32[]{:S(2)}) copy-start(f32[1,7,7,32,128]{4,3,2,1,0:T(8,128)} %coup_hbm.1) | copy-start | bytes 2408452
  32.0 50.4 %copy-start.6 = (f32[7,7,1024]{2,1,0:T(8,128)S(1)}, f32[7,7,1024]{2,1,0:T(8,128)}, u32[]{:S(2)}) copy-start(f32[7,7,1024]{2,1,0:T(8,128)} %pre_hbm.1) | copy-start | bytes 602116
  32.0 50.4 %copy-start.7 = (f32[7,7,1024]{2,1,0:T(8,128)S(1)}, f32[7,7,1024]{2,1,0:T(8,128)}, u32[]{:S(2)}) copy-start(f32[7,7,1024]{2,1,0:T(8,128)} %diag_hbm.1) | copy-start | bytes 602116
  32.1 50.4 %copy-start.8 = (f32[7,7,1024]{2,1,0:T(8,128)S(1)}, f32[7,7,1024]{2,1,0:T(8,128)}, u32[]{:S(2)}) copy-start(f32[7,7,1024]{2,1,0:T(8,128)} %low_hbm.1) | copy-start | bytes 602116
  32.1 50.4 %copy-start.14 = (s32[1,32,128]{2,1,0:T(8,128)S(1)}, s32[1,32,128]{2,1,0:T(8,128)}, u32[]{:S(2)}) copy-start(s32[1,32,128]{2,1,0:T(8,128)} %send_hbm.1) | copy-start | bytes 49156
  32.1 50.4 %copy-start.15 = (f32[7,1024]{1,0:T(8,128)S(1)}, f32[7,1024]{1,0:T(8,128)}, u32[]{:S(2)}) copy-start(f32[7,1024]{1,0:T(8,128)} %rhs_hbm.1) | copy-start | bytes 86020
  32.1 50.4 %copy-start.16 = (s32[1,32,128]{2,1,0:T(8,128)S(1)}, s32[1,32,128]{2,1,0:T(8,128)}, u32[]{:S(2)}) copy-start(s32[1,32,128]{2,1,0:T(8,128)} %cells_hbm.1) | copy-start | bytes 49156
  32.1 50.4 %copy-start.38 = (s32[1,32]{1,0:T(1,128)S(1)}, s32[1,32]{1,0:T(1,128)}, u32[]{:S(2)}) copy-start(s32[1,32]{1,0:T(1,128)} %halo_hbm.1) | copy-start | bytes 388

commit v3 on v2

--- a/solution.py
+++ b/solution.py
@@ -161,16 +161,14 @@
     for s in range(peers):
         x = recv_ref[s * 8 : (s + 1) * 8, :]
         first = x.astype(jnp.bfloat16).astype(jnp.float32)
-        rest = x - first
-        second = rest.astype(jnp.bfloat16).astype(jnp.float32)
-        third = rest - second
+        second = x - first
         cell = cells_ref[0, s : s + 1, :]
         low = jnp.broadcast_to(cell & (LANES - 1), (LANES, LANES))
         high = jnp.broadcast_to(cell >> 7, (8, LANES))
         pieces = []
         for t in range(tiles):
             here = high == t
-            pieces += [jnp.where(here, part, 0.0) for part in (first, second, third)]
+            pieces += [jnp.where(here, part, 0.0) for part in (first, second)]
         left.append(jnp.concatenate(pieces, axis=0).astype(jnp.bfloat16))
         right.append(jnp.where(spots == low, 1.0, 0.0).astype(jnp.bfloat16))
     total = lax.dot_general(
@@ -181,8 +179,7 @@
     )
     out = []
     for t in range(tiles):
-        a, b, c = (total[t * 24 + 8 * k : t * 24 + 8 * k + 8] for k in range(3))
-        out.append((c + b) + a)
+        out.append(total[t * 16 : t * 16 + 8] + total[t * 16 + 8 : t * 16 + 16])
     return jnp.concatenate(out, axis=1)
 
 
@@ -230,24 +227,26 @@
     rhs_ref, sems,
 ):
     whole = [(rhs_hbm, rhs_ref), (send_hbm, send_ref), (halo_hbm, halo_ref)]
-    rows = [(pre_hbm.at[i], pre_ref.at[i]) for i in range(F)]
-    faces = [(coup_hbm.at[0, i], coup_ref.at[0, i]) for i in range(F)]
+    rows = [(pre_hbm, pre_ref)]
+    faces = [(coup_hbm, coup_ref)]
     blocks = [(diag_hbm, diag_ref), (low_hbm, low_ref), (up_hbm, up_ref), (cells_hbm, cells_ref)]
     copies = [pltpu.make_async_copy(*pair, sems.at[k]) for k, pair in enumerate(whole + rows + faces + blocks)]
     for copy in copies:
         copy.start()
-    for copy in copies[: len(whole) + F]:
+    for copy in copies[: len(whole)]:
         copy.wait()
     u = jnp.concatenate([rhs_ref[...], jnp.zeros((1, rhs_ref.shape[1]), jnp.float32)], axis=0)
+    u_ref[...] = u
+    gram_ref[0], gram_ref[1] = products([u], u)
+    for copy in copies[len(whole) : len(whole) + 1]:
+        copy.wait()
     z = precondition(pre_ref, u)
-    u_ref[...] = u
     z_ref[...] = z
-    gram_ref[0], gram_ref[1] = products([u], u)
     taken = gather(z, send_ref)
-    for copy in copies[len(whole) + F : len(whole) + 2 * F]:
+    for copy in copies[len(whole) + 1 : len(whole) + 2]:
         copy.wait()
     mix(taken, coup_ref, halo_ref, msg_ref)
-    for copy in copies[len(whole) + 2 * F :]:
+    for copy in copies[len(whole) + 2 :]:
         copy.wait()
     y_ref[...] = local_part(z, diag_ref, low_ref, up_ref)
 
@@ -328,7 +327,7 @@
     for k in range(n):
         reach = reach + jnp.abs(coef[k][0]) * jnp.sqrt(norms[k])
     ok = ok & (reach * reach < 1e7 * left[0])
-    flag_ref[0] = jnp.min(jnp.where(ok, 1, 0))
+    flag_ref[...] = jnp.where(ok, 1, 0)
     cells = adj_ref.shape[1]
     weight = [jnp.broadcast_to(coef[k][0][:, :1], (8, cells)) for k in range(n)]
     adj = weight[0] * z_refs[0][...]
@@ -395,12 +394,12 @@
     got = lax.all_to_all(msg, BOTH, 0, 0, tiled=True)
     adjoint, residual, flag = call(
         functools.partial(finish_kernel, count),
-        (shape(fields, cells), shape(fields, cells), jax.ShapeDtypeStruct((1,), jnp.int32)),
+        (shape(fields, cells), shape(fields, cells), jax.ShapeDtypeStruct((1, LANES), jnp.int32)),
         got, *us, *zs,
         name="finish",
     )
     args, adjoint, residual, flag = lax.optimization_barrier((args, adjoint, residual, flag))
-    return lax.switch(flag[0], [lambda *_: arnoldi(*args), lambda *outs: outs], adjoint, residual)
+    return lax.switch(flag[0, 0], [lambda *_: arnoldi(*args), lambda *outs: outs], adjoint, residual)
 
 
 def solution(mesh):

time: 83.2 us -> 82 us (0.986)
  no operation moved by 1% of the time
where the time goes in v3:
time: 82 us; the launch traced here: 81.7 us
  blocking collectives  73.7 us (90%)
  Pallas kernels  6.65 us (8%)
  between operations  1.02 us (1%)
    all_to_all x4, blocking collectives, per_device(): lax.all_to_all(msg.reshape(peers, 8, LANES), 'blk', 0, 0, tiled=True)  50 us
    all_to_all x1, blocking collectives, per_device(): got = lax.all_to_all(msg, BOTH, 0, 0, tiled=True)  23.8 us
    pallas_call x6, Pallas kernels, call(): pl.pallas_call(kernel, out_shape=out, name=name, in_specs=[pl.BlockSpec(m...  6.65 us

profile of v3, /device:TPU:1, one launch (start us, length us, event | category | flops | bytes accessed | tf_op | source)
XLA Modules:
  0.0 81.7 jit_solution(5071662495052803571)
XLA Ops:
  0.6 1.8 %first.1 = (f32[8,1024]{1,0:T(8,128)S(1)}, f32[8,1024]{1,0:T(8,128)S(1)}, f32[256,128]{1,0:T(8,128)S(1)}, f32[8,1024]{1,0:T(8,128)S(1)}, f32[2,8,128]{2,1,0:T(8,...) custom-call(f32[7,1024]{1,0:T(8,128)} %rhs_hbm.1, ...), custom_call_target="tpu_custom_call" | custom-call | tf_op jit(solution)/shard_map/first/pallas_call | solution.py:347
  2.5 16.0 %all_to_all.51 = f32[32,8,128]{2,1,0:T(8,128)S(1)} all-to-all(f32[32,8,128]{2,1,0:T(8,128)S(1)} %bitcast.576), channel_id=1, replica_groups=mesh['blk'=32,'grp'=8] {'blk'}, dimensions={0} | all-to-all | bytes 262144 | tf_op jit(solution)/shard_map/all_to_all | solution.py:381
  18.5 1.0 %step.3 = (f32[8,1024]{1,0:T(8,128)S(1)}, f32[8,1024]{1,0:T(8,128)S(1)}, f32[256,128]{1,0:T(8,128)S(1)}, f32[8,1024]{1,0:T(8,128)S(1)}, f32[2,8,128]{2,1,0:T(8,128)S(1)}) custom-call(f32[256,128]{1,0:T(8,128)S(1)} %bitcast.571, s32[1,32,128]{2,1,0:T(8,128)S(1)} %get-tuple-element.176.cells_ref, f32[8,1024]{1,0:T(8,128)S(1)} %get-tuple-element.177.y_ref, ...), custom_call_target="tpu_custom_call" | custom-call | tf_op jit(solution)/shard_map/step/pallas_call | solution.py:347
  19.5 11.3 %all_to_all.52 = f32[32,8,128]{2,1,0:T(8,128)S(1)} all-to-all(f32[32,8,128]{2,1,0:T(8,128)S(1)} %bitcast.578), channel_id=1, replica_groups=mesh['blk'=32,'grp'=8] {'blk'}, dimensions={0} | all-to-all | bytes 262144 | tf_op jit(solution)/shard_map/all_to_all | solution.py:381
  30.7 1.0 %step.4 = (f32[8,1024]{1,0:T(8,128)S(1)}, f32[8,1024]{1,0:T(8,128)S(1)}, f32[256,128]{1,0:T(8,128)S(1)}, f32[8,1024]{1,0:T(8,128)S(1)}, f32[2,8,128]{2,1,0:T(8,128)S(1)}) custom-call(f32[256,128]{1,0:T(8,128)S(1)} %bitcast.572, s32[1,32,128]{2,1,0:T(8,128)S(1)} %get-tuple-element.176.cells_ref, f32[8,1024]{1,0:T(8,128)S(1)} %get-tuple-element.187.y_ref, ...), custom_call_target="tpu_custom_call" | custom-call | tf_op jit(solution)/shard_map/step/pallas_call | solution.py:347
  31.7 0.0 copy-start.5
  31.7 0.0 copy-start.6
  31.8 0.0 copy-start.7
  31.8 0.0 copy-start.8
  31.8 0.0 copy-start.14
  31.8 0.0 copy-start.15
  31.8 0.0 copy-start.16
  31.8 0.0 copy-start.38
  31.8 11.4 %all_to_all.53 = f32[32,8,128]{2,1,0:T(8,128)S(1)} all-to-all(f32[32,8,128]{2,1,0:T(8,128)S(1)} %bitcast.579), channel_id=1, replica_groups=mesh['blk'=32,'grp'=8] {'blk'}, dimensions={0} | all-to-all | bytes 262144 | tf_op jit(solution)/shard_map/all_to_all | solution.py:381
  43.2 1.0 %step.5 = (f32[8,1024]{1,0:T(8,128)S(1)}, f32[8,1024]{1,0:T(8,128)S(1)}, f32[256,128]{1,0:T(8,128)S(1)}, f32[8,1024]{1,0:T(8,128)S(1)}, f32[2,8,128]{2,1,0:T(8,128)S(1)}) custom-call(f32[256,128]{1,0:T(8,128)S(1)} %bitcast.570, s32[1,32,128]{2,1,0:T(8,128)S(1)} %get-tuple-element.176.cells_ref, f32[8,1024]{1,0:T(8,128)S(1)} %get-tuple-element.190.y_ref, ...), custom_call_target="tpu_custom_call" | custom-call | tf_op jit(solution)/shard_map/step/pallas_call | solution.py:347
  44.2 11.3 %all_to_all.54 = f32[32,8,128]{2,1,0:T(8,128)S(1)} all-to-all(f32[32,8,128]{2,1,0:T(8,128)S(1)} %bitcast.575), channel_id=1, replica_groups=mesh['blk'=32,'grp'=8] {'blk'}, dimensions={0} | all-to-all | bytes 262144 | tf_op jit(solution)/shard_map/all_to_all | solution.py:381
  55.5 0.8 last.1
  56.3 23.8 %all_to_all.55 = f32[256,1,128]{2,1,0:T(1,128)S(1)} all-to-all(f32[256,1,128]{2,1,0:T(1,128)S(1)} %bitcast.577), channel_id=1, replica_groups=mesh['blk'=32,'grp'=8] {'blk','grp'}, dimensions={0} | all-to-all | bytes 262144 | tf_op jit(solution)/shard_map/all_to_all | solution.py:394
  80.0 1.1 %finish.1 = (f32[7,1024]{1,0:T(8,128)}, f32[7,1024]{1,0:T(8,128)}, s32[1,128]{1,0:T(1,128)S(1)}) custom-call(f32[256,128]{1,0:T(8,128)S(1)} %bitcast.573, f32[8,1024]{1,0:T(8,128)S(1)} %get-tuple-element.185.refs_0_, f32[8,1024]{1,0:T(8,128)S(1)} %get-tuple-element.188.refs_1_, f32[8,1024]{1,0:T(8,128)S(1)} %get-tuple-element.191.refs_2_, ...), custom_call_target="tpu_custom_call" | custom-call | tf_op jit(solution)/shard_map/finish/pallas_call | solution.py:347
  81.2 0.0 copy-done.5
  81.2 0.0 copy-done.6
  81.2 0.0 copy-done.7
  81.2 0.0 copy-done.8
  81.2 0.0 copy-done.14
  81.2 0.0 copy-done.15
  81.3 0.0 copy-done.16
  81.3 0.0 copy-done.38
  81.3 0.2 conditional.1
Async XLA Ops:
  31.7 49.5 %copy-start.5 = (f32[1,7,7,32,128]{4,3,2,1,0:T(8,128)S(1)}, f32[1,7,7,32,128]{4,3,2,1,0:T(8,128)}, u32[]{:S(2)}) copy-start(f32[1,7,7,32,128]{4,3,2,1,0:T(8,128)} %coup_hbm.1) | copy-start | bytes 2408452
  31.7 49.5 %copy-start.6 = (f32[7,7,1024]{2,1,0:T(8,128)S(1)}, f32[7,7,1024]{2,1,0:T(8,128)}, u32[]{:S(2)}) copy-start(f32[7,7,1024]{2,1,0:T(8,128)} %pre_hbm.1) | copy-start | bytes 602116
  31.8 49.5 %copy-start.7 = (f32[7,7,1024]{2,1,0:T(8,128)S(1)}, f32[7,7,1024]{2,1,0:T(8,128)}, u32[]{:S(2)}) copy-start(f32[7,7,1024]{2,1,0:T(8,128)} %diag_hbm.1) | copy-start | bytes 602116
  31.8 49.5 %copy-start.8 = (f32[7,7,1024]{2,1,0:T(8,128)S(1)}, f32[7,7,1024]{2,1,0:T(8,128)}, u32[]{:S(2)}) copy-start(f32[7,7,1024]{2,1,0:T(8,128)} %low_hbm.1) | copy-start | bytes 602116
  31.8 49.5 %copy-start.14 = (s32[1,32,128]{2,1,0:T(8,128)S(1)}, s32[1,32,128]{2,1,0:T(8,128)}, u32[]{:S(2)}) copy-start(s32[1,32,128]{2,1,0:T(8,128)} %send_hbm.1) | copy-start | bytes 49156
  31.8 49.5 %copy-start.15 = (f32[7,1024]{1,0:T(8,128)S(1)}, f32[7,1024]{1,0:T(8,128)}, u32[]{:S(2)}) copy-start(f32[7,1024]{1,0:T(8,128)} %rhs_hbm.1) | copy-start | bytes 86020
  31.8 49.5 %copy-start.16 = (s32[1,32,128]{2,1,0:T(8,128)S(1)}, s32[1,32,128]{2,1,0:T(8,128)}, u32[]{:S(2)}) copy-start(s32[1,32,128]{2,1,0:T(8,128)} %cells_hbm.1) | copy-start | bytes 49156
  31.8 49.5 %copy-start.38 = (s32[1,32]{1,0:T(1,128)S(1)}, s32[1,32]{1,0:T(1,128)}, u32[]{:S(2)}) copy-start(s32[1,32]{1,0:T(1,128)} %halo_hbm.1) | copy-start | bytes 388

commit v4 on v3

--- a/solution.py
+++ b/solution.py
@@ -1,4 +1,5 @@
 import functools
+import math
 
 import jax
 import jax.numpy as jnp
@@ -263,7 +264,7 @@
 
 
 def last_kernel(recv_ref, cells_ref, y_ref, *refs):
-    u_refs, gram_refs, (u_ref, msg_ref) = refs[:ITERS], refs[ITERS : 2 * ITERS], refs[2 * ITERS :]
+    u_refs, gram_refs, (u_ref, row_ref) = refs[:ITERS], refs[ITERS : 2 * ITERS], refs[2 * ITERS :]
     u = y_ref[...] + scatter(recv_ref, cells_ref, y_ref.shape[1] // LANES)
     u_ref[...] = u
     columns = [(ref[0], ref[1]) for ref in gram_refs]
@@ -274,8 +275,14 @@
     for j in range(ITERS + 1):
         for part, total in enumerate(lane_sum(*columns[j])):
             placed = jnp.where(lane == row + (part * 64 + 8 * j), total, placed)
-    placed = jnp.sum(placed, axis=0, keepdims=True)
-    msg_ref[...] = jnp.broadcast_to(placed, msg_ref.shape)
+    row_ref[...] = jnp.broadcast_to(jnp.sum(placed, axis=0, keepdims=True), row_ref.shape)
+
+
+def pair_kernel(own_ref, other_ref, msg_ref):
+    total, error = two_sum(own_ref[...], other_ref[...])
+    lane = lax.broadcasted_iota(jnp.int32, total.shape, 1)
+    row = jnp.where(lane < 64, total, total + pltpu.roll(error, 64, 1))
+    msg_ref[...] = jnp.concatenate([row] * (msg_ref.shape[0] // 8), axis=0)
 
 
 def finish_kernel(count, got_ref, *refs):
@@ -357,10 +364,22 @@
     )(*args)
 
 
+def core_groups(blk, grp):
+    side = math.isqrt(blk // 2)
+
+    def distance(chip):
+        place, z = chip
+        return sum(min(at, size - at) for at, size in ((place // side, side), (place % side, side), (z, grp)))
+
+    chips = sorted(((place, z) for place in range(blk // 2) for z in range(grp)), key=lambda c: (distance(c), c))
+    chips = chips[-1:] + chips[:-1]
+    return [[(place * 2 + core) * grp + z for place, z in chips] for core in range(2)]
+
+
 def per_device(rhs, diag_blocks, lower_blocks, upper_blocks, precond, coupling, send_cells, recv_cells, halo_len):
     fields, cells = rhs.shape
     peers = send_cells.shape[1]
-    count = peers * lax.axis_size("grp")
+    count = peers * lax.axis_size("grp") // 2
     vector = shape(8, cells)
     message = shape(peers * 8, LANES)
     args = (rhs, diag_blocks, lower_blocks, upper_blocks, precond, coupling, send_cells, recv_cells, halo_len)
@@ -389,9 +408,12 @@
             zs.append(z)
             grams.append(gram)
         else:
-            u, msg = call(last_kernel, (vector, shape(count, LANES)), got, recv_cells, y, *us, *grams, name="last")
+            u, row = call(last_kernel, (vector, shape(8, LANES)), got, recv_cells, y, *us, *grams, name="last")
         us.append(u)
-    got = lax.all_to_all(msg, BOTH, 0, 0, tiled=True)
+    other = lax.ppermute(row, "blk", [(i, i ^ 1) for i in range(peers)])
+    (msg,) = call(pair_kernel, (shape(count, LANES),), row, other, name="pair")
+    groups = core_groups(peers, lax.axis_size("grp"))
+    got = lax.all_to_all(msg, BOTH, 0, 0, axis_index_groups=groups, tiled=True)
     adjoint, residual, flag = call(
         functools.partial(finish_kernel, count),
         (shape(fields, cells), shape(fields, cells), jax.ShapeDtypeStruct((1, LANES), jnp.int32)),

time: 82 us -> 77.5 us (0.945)
  blocking collectives: 73.7 us -> 67.9 us
    all_to_all x1, blocking collectives: 23.8 us -> 17.9 us  [per_device(): got = lax.all_to_all(msg, BOTH, 0, 0, axis_index_groups=groups, tiled=True)]
    ppermute x0 -> x1, waiting for transfers between devices: none -> 0.82 us  [per_device(): other = lax.ppermute(row, 'blk', [(i, i ^ 1) for i in range(peers)])]
    pallas_call x6 -> x7, Pallas kernels: 6.65 us -> 6.63 us  [call(): pl.pallas_call(kernel, out_shape=out, name=name, in_specs=[pl.BlockSpec(m...]
  transfers between devices with their start and end apart: 0 -> 1, of which waited for: 0 -> 1; matrix products, arithmetic and copies ran while one was open for 0% -> 0% of each run, Pallas kernels for 0% -> 0%
where the time goes in v4:
time: 77.5 us; the launch traced here: 77.1 us
  blocking collectives  67.9 us (88%)
  Pallas kernels  6.63 us (9%)
  between operations  1.02 us (1%)
  waiting for transfers between devices  0.82 us (1%)
    all_to_all x4, blocking collectives, per_device(): lax.all_to_all(msg.reshape(peers, 8, LANES), 'blk', 0, 0, tiled=True)  50 us
    all_to_all x1, blocking collectives, per_device(): got = lax.all_to_all(msg, BOTH, 0, 0, axis_index_groups=groups, tiled=True)  17.9 us
    pallas_call x7, Pallas kernels, call(): pl.pallas_call(kernel, out_shape=out, name=name, in_specs=[pl.BlockSpec(m...  6.63 us
  transfers between devices with their start and end apart: 1, of which 1 were waited for; matrix products, arithmetic and copies ran while one was open for 0% of the time, Pallas kernels for 0%

profile of v4, /device:TPU:1, one launch (start us, length us, event | category | flops | bytes accessed | tf_op | source)
XLA Modules:
  0.0 77.1 jit_solution(3288489724367495419)
XLA Ops:
  0.6 1.8 %first.1 = (f32[8,1024]{1,0:T(8,128)S(1)}, f32[8,1024]{1,0:T(8,128)S(1)}, f32[256,128]{1,0:T(8,128)S(1)}, f32[8,1024]{1,0:T(8,128)S(1)}, f32[2,8,128]{2,1,0:T(8,...) custom-call(f32[7,1024]{1,0:T(8,128)} %rhs_hbm.1, ...), custom_call_target="tpu_custom_call" | custom-call | tf_op jit(solution)/shard_map/first/pallas_call | solution.py:354
  2.5 16.0 %all_to_all.51 = f32[32,8,128]{2,1,0:T(8,128)S(1)} all-to-all(f32[32,8,128]{2,1,0:T(8,128)S(1)} %bitcast.577), channel_id=1, replica_groups=mesh['blk'=32,'grp'=8] {'blk'}, dimensions={0} | all-to-all | bytes 262144 | tf_op jit(solution)/shard_map/all_to_all | solution.py:400
  18.5 1.0 %step.3 = (f32[8,1024]{1,0:T(8,128)S(1)}, f32[8,1024]{1,0:T(8,128)S(1)}, f32[256,128]{1,0:T(8,128)S(1)}, f32[8,1024]{1,0:T(8,128)S(1)}, f32[2,8,128]{2,1,0:T(8,128)S(1)}) custom-call(f32[256,128]{1,0:T(8,128)S(1)} %bitcast.571, s32[1,32,128]{2,1,0:T(8,128)S(1)} %get-tuple-element.176.cells_ref, f32[8,1024]{1,0:T(8,128)S(1)} %get-tuple-element.177.y_ref, ...), custom_call_target="tpu_custom_call" | custom-call | tf_op jit(solution)/shard_map/step/pallas_call | solution.py:354
  19.5 11.3 %all_to_all.52 = f32[32,8,128]{2,1,0:T(8,128)S(1)} all-to-all(f32[32,8,128]{2,1,0:T(8,128)S(1)} %bitcast.578), channel_id=1, replica_groups=mesh['blk'=32,'grp'=8] {'blk'}, dimensions={0} | all-to-all | bytes 262144 | tf_op jit(solution)/shard_map/all_to_all | solution.py:400
  30.7 1.0 %step.4 = (f32[8,1024]{1,0:T(8,128)S(1)}, f32[8,1024]{1,0:T(8,128)S(1)}, f32[256,128]{1,0:T(8,128)S(1)}, f32[8,1024]{1,0:T(8,128)S(1)}, f32[2,8,128]{2,1,0:T(8,128)S(1)}) custom-call(f32[256,128]{1,0:T(8,128)S(1)} %bitcast.572, s32[1,32,128]{2,1,0:T(8,128)S(1)} %get-tuple-element.176.cells_ref, f32[8,1024]{1,0:T(8,128)S(1)} %get-tuple-element.187.y_ref, ...), custom_call_target="tpu_custom_call" | custom-call | tf_op jit(solution)/shard_map/step/pallas_call | solution.py:354
  31.7 0.0 copy-start.5
  31.7 0.0 copy-start.6
  31.7 0.0 copy-start.7
  31.7 0.0 copy-start.8
  31.8 0.0 copy-start.14
  31.8 0.0 copy-start.15
  31.8 0.0 copy-start.16
  31.8 0.0 copy-start.38
  31.8 11.4 %all_to_all.53 = f32[32,8,128]{2,1,0:T(8,128)S(1)} all-to-all(f32[32,8,128]{2,1,0:T(8,128)S(1)} %bitcast.579), channel_id=1, replica_groups=mesh['blk'=32,'grp'=8] {'blk'}, dimensions={0} | all-to-all | bytes 262144 | tf_op jit(solution)/shard_map/all_to_all | solution.py:400
  43.2 1.0 %step.5 = (f32[8,1024]{1,0:T(8,128)S(1)}, f32[8,1024]{1,0:T(8,128)S(1)}, f32[256,128]{1,0:T(8,128)S(1)}, f32[8,1024]{1,0:T(8,128)S(1)}, f32[2,8,128]{2,1,0:T(8,128)S(1)}) custom-call(f32[256,128]{1,0:T(8,128)S(1)} %bitcast.570, s32[1,32,128]{2,1,0:T(8,128)S(1)} %get-tuple-element.176.cells_ref, f32[8,1024]{1,0:T(8,128)S(1)} %get-tuple-element.190.y_ref, ...), custom_call_target="tpu_custom_call" | custom-call | tf_op jit(solution)/shard_map/step/pallas_call | solution.py:354
  44.2 11.3 %all_to_all.54 = f32[32,8,128]{2,1,0:T(8,128)S(1)} all-to-all(f32[32,8,128]{2,1,0:T(8,128)S(1)} %bitcast.576), channel_id=1, replica_groups=mesh['blk'=32,'grp'=8] {'blk'}, dimensions={0} | all-to-all | bytes 262144 | tf_op jit(solution)/shard_map/all_to_all | solution.py:400
  55.5 0.7 last.1
  56.2 0.5 collective-permute-start
  56.7 0.8 %collective-permute-done.other_ref = f32[8,128]{1,0:T(8,128)S(1)} collective-permute-done((f32[8,128]{1,0:T(8,128)S(1)}, f32[8,128]{1,0:T(8,128)S(1)}, u32[]{:S(2)}, u32[]{:S(2)}) %collective-permute-start) | collective-permute-done | bytes 4128 | tf_op jit(solution)/shard_map/ppermute | solution.py:413
  57.5 0.1 pair.1
  57.6 17.9 %all_to_all.55 = f32[128,1,128]{2,1,0:T(1,128)S(1)} all-to-all(f32[128,1,128]{2,1,0:T(1,128)S(1)} %bitcast.574), channel_id=1, replica_groups={{164,0,1,7,16,48,64,192,2,6,17,23,32,49,55,65,71,80,112,128,193,199,208..., dimensions={0} | all-to-all | bytes 131072 | tf_op jit(solution)/shard_map/all_to_all | solution.py:416
  75.5 1.1 %finish.1 = (f32[7,1024]{1,0:T(8,128)}, f32[7,1024]{1,0:T(8,128)}, s32[1,128]{1,0:T(1,128)S(1)}) custom-call(f32[128,128]{1,0:T(8,128)S(1)} %bitcast.575, f32[8,1024]{1,0:T(8,128)S(1)} %get-tuple-element.185.refs_0_, f32[8,1024]{1,0:T(8,128)S(1)} %get-tuple-element.188.refs_1_, f32[8,1024]{1,0:T(8,128)S(1)} %get-tuple-element.191.refs_2_, ...), custom_call_target="tpu_custom_call" | custom-call | tf_op jit(solution)/shard_map/finish/pallas_call | solution.py:354
  76.6 0.0 copy-done.5
  76.6 0.0 copy-done.6
  76.6 0.0 copy-done.7
  76.6 0.0 copy-done.8
  76.6 0.0 copy-done.14
  76.7 0.0 copy-done.15
  76.7 0.0 copy-done.16
  76.7 0.0 copy-done.38
  76.7 0.2 conditional.1
Async XLA Ops:
  31.7 44.9 %copy-start.5 = (f32[1,7,7,32,128]{4,3,2,1,0:T(8,128)S(1)}, f32[1,7,7,32,128]{4,3,2,1,0:T(8,128)}, u32[]{:S(2)}) copy-start(f32[1,7,7,32,128]{4,3,2,1,0:T(8,128)} %coup_hbm.1) | copy-start | bytes 2408452
  31.7 44.9 %copy-start.6 = (f32[7,7,1024]{2,1,0:T(8,128)S(1)}, f32[7,7,1024]{2,1,0:T(8,128)}, u32[]{:S(2)}) copy-start(f32[7,7,1024]{2,1,0:T(8,128)} %pre_hbm.1) | copy-start | bytes 602116
  31.7 44.9 %copy-start.7 = (f32[7,7,1024]{2,1,0:T(8,128)S(1)}, f32[7,7,1024]{2,1,0:T(8,128)}, u32[]{:S(2)}) copy-start(f32[7,7,1024]{2,1,0:T(8,128)} %diag_hbm.1) | copy-start | bytes 602116
  31.7 44.9 %copy-start.8 = (f32[7,7,1024]{2,1,0:T(8,128)S(1)}, f32[7,7,1024]{2,1,0:T(8,128)}, u32[]{:S(2)}) copy-start(f32[7,7,1024]{2,1,0:T(8,128)} %low_hbm.1) | copy-start | bytes 602116
  31.8 44.9 %copy-start.14 = (s32[1,32,128]{2,1,0:T(8,128)S(1)}, s32[1,32,128]{2,1,0:T(8,128)}, u32[]{:S(2)}) copy-start(s32[1,32,128]{2,1,0:T(8,128)} %send_hbm.1) | copy-start | bytes 49156
  31.8 44.9 %copy-start.15 = (f32[7,1024]{1,0:T(8,128)S(1)}, f32[7,1024]{1,0:T(8,128)}, u32[]{:S(2)}) copy-start(f32[7,1024]{1,0:T(8,128)} %rhs_hbm.1) | copy-start | bytes 86020
  31.8 44.9 %copy-start.16 = (s32[1,32,128]{2,1,0:T(8,128)S(1)}, s32[1,32,128]{2,1,0:T(8,128)}, u32[]{:S(2)}) copy-start(s32[1,32,128]{2,1,0:T(8,128)} %cells_hbm.1) | copy-start | bytes 49156
  31.8 44.9 %copy-start.38 = (s32[1,32]{1,0:T(1,128)S(1)}, s32[1,32]{1,0:T(1,128)}, u32[]{:S(2)}) copy-start(s32[1,32]{1,0:T(1,128)} %halo_hbm.1) | copy-start | bytes 388
  56.2 1.3 %collective-permute-start = (f32[8,128]{1,0:T(8,128)S(1)}, f32[8,128]{1,0:T(8,128)S(1)}, u32[]{:S(2)}, u32[]{:S(2)}) collective-permute-start(f32[8,128]{1,0:T(8,128)S(1)} %get-tuple-element.199.own_ref), channel_id=1, source_target_pairs={{0,8},{8,0},{16,24},{24,16},{32,40},{40,32},{48,56},{56,48},{64,72... | collective-permute-start | bytes 12296 | tf_op jit(solution)/shard_map/ppermute | solution.py:413

commit v5 on v4

--- a/solution.py
+++ b/solution.py
@@ -107,6 +107,11 @@
     return quick_sum(q, rest[0] * inverse)
 
 
+def far_place(blk):
+    side = math.isqrt(blk // 2)
+    return (side // 2) * (side + 1) * 2
+
+
 def row_sums(parts):
     rows = [jnp.sum(part, axis=0, keepdims=True) for part in parts]
     return jnp.concatenate(rows + [jnp.zeros_like(rows[0])], axis=0)
@@ -151,7 +156,10 @@
             total = coup_ref[0, i, 0, q * 8 : (q + 1) * 8, :] * taken[q][0]
             for j in range(1, F):
                 total = total + coup_ref[0, i, j, q * 8 : (q + 1) * 8, :] * taken[q][j]
-            msg_ref[pl.ds(q * 64 + i, 8, stride=8), :] = jnp.where(live, total, 0.0)
+            total = jnp.where(live, total, 0.0)
+            for half in (0, 4):
+                place = (q * 8 + half) ^ far_place(peers)
+                msg_ref[pl.ds(place * 8 + i, 4, stride=8), :] = total[half : half + 4]
         msg_ref[pl.ds(q * 64 + F, 8, stride=8), :] = jnp.zeros((8, LANES), jnp.float32)
 
 
@@ -163,7 +171,8 @@
         x = recv_ref[s * 8 : (s + 1) * 8, :]
         first = x.astype(jnp.bfloat16).astype(jnp.float32)
         second = x - first
-        cell = cells_ref[0, s : s + 1, :]
+        source = s ^ far_place(peers)
+        cell = cells_ref[0, source : source + 1, :]
         low = jnp.broadcast_to(cell & (LANES - 1), (LANES, LANES))
         high = jnp.broadcast_to(cell >> 7, (8, LANES))
         pieces = []
@@ -396,8 +405,10 @@
     )
     face, blocks, recv_cells = kept[:4], kept[4:7], kept[7]
     us, zs, grams = [u], [z], [gram]
+    order = [i ^ far_place(peers) for i in range(peers)]
     for col in range(ITERS):
-        got = lax.all_to_all(msg.reshape(peers, 8, LANES), "blk", 0, 0, tiled=True).reshape(peers * 8, LANES)
+        got = lax.all_to_all(msg.reshape(peers, 8, LANES), "blk", 0, 0, axis_index_groups=[order], tiled=True)
+        got = got.reshape(peers * 8, LANES)
         if col < ITERS - 1:
             u, z, msg, y, gram = call(
                 functools.partial(step_kernel, col + 1),

time: 77.5 us -> 74 us (0.955)
  blocking collectives: 67.9 us -> 64.3 us
    all_to_all x4, blocking collectives: 50 us -> 45.7 us  [per_device(): lax.all_to_all(msg.reshape(peers, 8, LANES), 'blk', 0, 0, axis_index_grou...]
where the time goes in v5:
time: 74 us; the launch traced here: 73.6 us
  blocking collectives  64.3 us (87%)
  Pallas kernels  6.65 us (9%)
  between operations  1.01 us (1%)
  waiting for transfers between devices  0.82 us (1%)
    all_to_all x4, blocking collectives, per_device(): lax.all_to_all(msg.reshape(peers, 8, LANES), 'blk', 0, 0, axis_index_grou...  45.7 us
    all_to_all x1, blocking collectives, per_device(): got = lax.all_to_all(msg, BOTH, 0, 0, axis_index_groups=groups, tiled=True)  18.6 us
    pallas_call x7, Pallas kernels, call(): pl.pallas_call(kernel, out_shape=out, name=name, in_specs=[pl.BlockSpec(m...  6.65 us
  transfers between devices with their start and end apart: 1, of which 1 were waited for; matrix products, arithmetic and copies ran while one was open for 0% of the time, Pallas kernels for 0%

profile of v5, /device:TPU:1, one launch (start us, length us, event | category | flops | bytes accessed | tf_op | source)
XLA Modules:
  0.0 73.6 jit_solution(15135972719662566675)
XLA Ops:
  0.6 1.8 %first.1 = (f32[8,1024]{1,0:T(8,128)S(1)}, f32[8,1024]{1,0:T(8,128)S(1)}, f32[256,128]{1,0:T(8,128)S(1)}, f32[8,1024]{1,0:T(8,128)S(1)}, f32[2,8,128]{2,1,0:T(8,...) custom-call(f32[7,1024]{1,0:T(8,128)} %rhs_hbm.1, ...), custom_call_target="tpu_custom_call" | custom-call | tf_op jit(solution)/shard_map/first/pallas_call | solution.py:363
  2.5 12.9 %all_to_all.51 = f32[32,8,128]{2,1,0:T(8,128)S(1)} all-to-all(f32[32,8,128]{2,1,0:T(8,128)S(1)} %bitcast.577), channel_id=1, replica_groups={{160,168,176,184,128,136,144,152,224,232,240,248,192,200,208,216,32,40,..., dimensions={0} | all-to-all | bytes 262144 | tf_op jit(solution)/shard_map/all_to_all | solution.py:410
  15.3 1.0 %step.3 = (f32[8,1024]{1,0:T(8,128)S(1)}, f32[8,1024]{1,0:T(8,128)S(1)}, f32[256,128]{1,0:T(8,128)S(1)}, f32[8,1024]{1,0:T(8,128)S(1)}, f32[2,8,128]{2,1,0:T(8,128)S(1)}) custom-call(f32[256,128]{1,0:T(8,128)S(1)} %bitcast.571, s32[1,32,128]{2,1,0:T(8,128)S(1)} %get-tuple-element.176.cells_ref, f32[8,1024]{1,0:T(8,128)S(1)} %get-tuple-element.177.y_ref, ...), custom_call_target="tpu_custom_call" | custom-call | tf_op jit(solution)/shard_map/step/pallas_call | solution.py:363
  16.3 10.9 %all_to_all.52 = f32[32,8,128]{2,1,0:T(8,128)S(1)} all-to-all(f32[32,8,128]{2,1,0:T(8,128)S(1)} %bitcast.578), channel_id=1, replica_groups={{160,168,176,184,128,136,144,152,224,232,240,248,192,200,208,216,32,40,..., dimensions={0} | all-to-all | bytes 262144 | tf_op jit(solution)/shard_map/all_to_all | solution.py:410
  27.2 1.0 %step.4 = (f32[8,1024]{1,0:T(8,128)S(1)}, f32[8,1024]{1,0:T(8,128)S(1)}, f32[256,128]{1,0:T(8,128)S(1)}, f32[8,1024]{1,0:T(8,128)S(1)}, f32[2,8,128]{2,1,0:T(8,128)S(1)}) custom-call(f32[256,128]{1,0:T(8,128)S(1)} %bitcast.572, s32[1,32,128]{2,1,0:T(8,128)S(1)} %get-tuple-element.176.cells_ref, f32[8,1024]{1,0:T(8,128)S(1)} %get-tuple-element.187.y_ref, ...), custom_call_target="tpu_custom_call" | custom-call | tf_op jit(solution)/shard_map/step/pallas_call | solution.py:363
  28.2 0.0 copy-start.5
  28.2 0.0 copy-start.6
  28.2 0.0 copy-start.7
  28.2 0.0 copy-start.8
  28.2 0.0 copy-start.14
  28.2 0.0 copy-start.15
  28.3 0.0 copy-start.16
  28.3 0.0 copy-start.38
  28.3 11.0 %all_to_all.53 = f32[32,8,128]{2,1,0:T(8,128)S(1)} all-to-all(f32[32,8,128]{2,1,0:T(8,128)S(1)} %bitcast.579), channel_id=1, replica_groups={{160,168,176,184,128,136,144,152,224,232,240,248,192,200,208,216,32,40,..., dimensions={0} | all-to-all | bytes 262144 | tf_op jit(solution)/shard_map/all_to_all | solution.py:410
  39.3 1.0 %step.5 = (f32[8,1024]{1,0:T(8,128)S(1)}, f32[8,1024]{1,0:T(8,128)S(1)}, f32[256,128]{1,0:T(8,128)S(1)}, f32[8,1024]{1,0:T(8,128)S(1)}, f32[2,8,128]{2,1,0:T(8,128)S(1)}) custom-call(f32[256,128]{1,0:T(8,128)S(1)} %bitcast.570, s32[1,32,128]{2,1,0:T(8,128)S(1)} %get-tuple-element.176.cells_ref, f32[8,1024]{1,0:T(8,128)S(1)} %get-tuple-element.190.y_ref, ...), custom_call_target="tpu_custom_call" | custom-call | tf_op jit(solution)/shard_map/step/pallas_call | solution.py:363
  40.3 10.9 %all_to_all.54 = f32[32,8,128]{2,1,0:T(8,128)S(1)} all-to-all(f32[32,8,128]{2,1,0:T(8,128)S(1)} %bitcast.576), channel_id=1, replica_groups={{160,168,176,184,128,136,144,152,224,232,240,248,192,200,208,216,32,40,..., dimensions={0} | all-to-all | bytes 262144 | tf_op jit(solution)/shard_map/all_to_all | solution.py:410
  51.2 0.7 last.1
  51.9 0.5 collective-permute-start
  52.4 0.8 %collective-permute-done.other_ref = f32[8,128]{1,0:T(8,128)S(1)} collective-permute-done((f32[8,128]{1,0:T(8,128)S(1)}, f32[8,128]{1,0:T(8,128)S(1)}, u32[]{:S(2)}, u32[]{:S(2)}) %collective-permute-start) | collective-permute-done | bytes 4128 | tf_op jit(solution)/shard_map/ppermute | solution.py:424
  53.2 0.1 pair.1
  53.3 18.6 %all_to_all.55 = f32[128,1,128]{2,1,0:T(1,128)S(1)} all-to-all(f32[128,1,128]{2,1,0:T(1,128)S(1)} %bitcast.574), channel_id=1, replica_groups={{164,0,1,7,16,48,64,192,2,6,17,23,32,49,55,65,71,80,112,128,193,199,208..., dimensions={0} | all-to-all | bytes 131072 | tf_op jit(solution)/shard_map/all_to_all | solution.py:427
  72.0 1.1 %finish.1 = (f32[7,1024]{1,0:T(8,128)}, f32[7,1024]{1,0:T(8,128)}, s32[1,128]{1,0:T(1,128)S(1)}) custom-call(f32[128,128]{1,0:T(8,128)S(1)} %bitcast.575, f32[8,1024]{1,0:T(8,128)S(1)} %get-tuple-element.185.refs_0_, f32[8,1024]{1,0:T(8,128)S(1)} %get-tuple-element.188.refs_1_, f32[8,1024]{1,0:T(8,128)S(1)} %get-tuple-element.191.refs_2_, ...), custom_call_target="tpu_custom_call" | custom-call | tf_op jit(solution)/shard_map/finish/pallas_call | solution.py:363
  73.1 0.0 copy-done.5
  73.1 0.0 copy-done.6
  73.1 0.0 copy-done.7
  73.1 0.0 copy-done.8
  73.1 0.0 copy-done.14
  73.1 0.0 copy-done.15
  73.2 0.0 copy-done.16
  73.2 0.0 copy-done.38
  73.2 0.2 conditional.1
Async XLA Ops:
  28.2 44.9 %copy-start.5 = (f32[1,7,7,32,128]{4,3,2,1,0:T(8,128)S(1)}, f32[1,7,7,32,128]{4,3,2,1,0:T(8,128)}, u32[]{:S(2)}) copy-start(f32[1,7,7,32,128]{4,3,2,1,0:T(8,128)} %coup_hbm.1) | copy-start | bytes 2408452
  28.2 44.9 %copy-start.6 = (f32[7,7,1024]{2,1,0:T(8,128)S(1)}, f32[7,7,1024]{2,1,0:T(8,128)}, u32[]{:S(2)}) copy-start(f32[7,7,1024]{2,1,0:T(8,128)} %pre_hbm.1) | copy-start | bytes 602116
  28.2 44.9 %copy-start.7 = (f32[7,7,1024]{2,1,0:T(8,128)S(1)}, f32[7,7,1024]{2,1,0:T(8,128)}, u32[]{:S(2)}) copy-start(f32[7,7,1024]{2,1,0:T(8,128)} %diag_hbm.1) | copy-start | bytes 602116
  28.2 44.9 %copy-start.8 = (f32[7,7,1024]{2,1,0:T(8,128)S(1)}, f32[7,7,1024]{2,1,0:T(8,128)}, u32[]{:S(2)}) copy-start(f32[7,7,1024]{2,1,0:T(8,128)} %low_hbm.1) | copy-start | bytes 602116
  28.2 44.9 %copy-start.14 = (s32[1,32,128]{2,1,0:T(8,128)S(1)}, s32[1,32,128]{2,1,0:T(8,128)}, u32[]{:S(2)}) copy-start(s32[1,32,128]{2,1,0:T(8,128)} %send_hbm.1) | copy-start | bytes 49156
  28.2 44.9 %copy-start.15 = (f32[7,1024]{1,0:T(8,128)S(1)}, f32[7,1024]{1,0:T(8,128)}, u32[]{:S(2)}) copy-start(f32[7,1024]{1,0:T(8,128)} %rhs_hbm.1) | copy-start | bytes 86020
  28.3 44.9 %copy-start.16 = (s32[1,32,128]{2,1,0:T(8,128)S(1)}, s32[1,32,128]{2,1,0:T(8,128)}, u32[]{:S(2)}) copy-start(s32[1,32,128]{2,1,0:T(8,128)} %cells_hbm.1) | copy-start | bytes 49156
  28.3 44.9 %copy-start.38 = (s32[1,32]{1,0:T(1,128)S(1)}, s32[1,32]{1,0:T(1,128)}, u32[]{:S(2)}) copy-start(s32[1,32]{1,0:T(1,128)} %halo_hbm.1) | copy-start | bytes 388
  51.9 1.3 %collective-permute-start = (f32[8,128]{1,0:T(8,128)S(1)}, f32[8,128]{1,0:T(8,128)S(1)}, u32[]{:S(2)}, u32[]{:S(2)}) collective-permute-start(f32[8,128]{1,0:T(8,128)S(1)} %get-tuple-element.199.own_ref), channel_id=1, source_target_pairs={{0,8},{8,0},{16,24},{24,16},{32,40},{40,32},{48,56},{56,48},{64,72... | collective-permute-start | bytes 12296 | tf_op jit(solution)/shard_map/ppermute | solution.py:424

commit v6 on v5

--- a/solution.py
+++ b/solution.py
@@ -109,7 +109,15 @@
 
 def far_place(blk):
     side = math.isqrt(blk // 2)
-    return (side // 2) * (side + 1) * 2
+    return (side // 2) * (side + 1) * 2 + 1
+
+
+def flip(value, bits):
+    half, bit = bits & 4, bits & 3
+    if bit == 0:
+        return pltpu.roll(value, half, 0) if half else value
+    rows = lax.broadcasted_iota(jnp.int32, value.shape, 0)
+    return jnp.where((rows & bit) == 0, pltpu.roll(value, 8 - bit - half, 0), pltpu.roll(value, bit + half, 0))
 
 
 def row_sums(parts):
@@ -145,6 +153,7 @@
 
 def mix(taken, coup_ref, halo_ref, msg_ref):
     peers = halo_ref.shape[1]
+    far = far_place(peers)
     lanes = lax.broadcasted_iota(jnp.int32, (8, LANES), 1)
     rows = lax.broadcasted_iota(jnp.int32, (8, peers), 0)
     cols = lax.broadcasted_iota(jnp.int32, (8, peers), 1)
@@ -152,14 +161,12 @@
     for q in range(peers // 8):
         size = jnp.sum(jnp.where(cols == rows + q * 8, lens, 0), axis=1, keepdims=True)
         live = lanes < size
+        place = (q * 8) ^ (far & ~7)
         for i in range(F):
             total = coup_ref[0, i, 0, q * 8 : (q + 1) * 8, :] * taken[q][0]
             for j in range(1, F):
                 total = total + coup_ref[0, i, j, q * 8 : (q + 1) * 8, :] * taken[q][j]
-            total = jnp.where(live, total, 0.0)
-            for half in (0, 4):
-                place = (q * 8 + half) ^ far_place(peers)
-                msg_ref[pl.ds(place * 8 + i, 4, stride=8), :] = total[half : half + 4]
+            msg_ref[pl.ds(place * 8 + i, 8, stride=8), :] = flip(jnp.where(live, total, 0.0), far & 7)
         msg_ref[pl.ds(q * 64 + F, 8, stride=8), :] = jnp.zeros((8, LANES), jnp.float32)
 
 

time: 74 us -> 73.2 us (0.989)
    all_to_all x4, blocking collectives: 45.7 us -> 44.9 us  [per_device(): lax.all_to_all(msg.reshape(peers, 8, LANES), 'blk', 0, 0, axis_index_grou...]
where the time goes in v6:
time: 73.2 us; the launch traced here: 72.8 us
  blocking collectives  63.6 us (87%)
  Pallas kernels  6.67 us (9%)
  between operations  1.02 us (1%)
  waiting for transfers between devices  0.82 us (1%)
    all_to_all x4, blocking collectives, per_device(): lax.all_to_all(msg.reshape(peers, 8, LANES), 'blk', 0, 0, axis_index_grou...  44.9 us
    all_to_all x1, blocking collectives, per_device(): got = lax.all_to_all(msg, BOTH, 0, 0, axis_index_groups=groups, tiled=True)  18.7 us
    pallas_call x7, Pallas kernels, call(): pl.pallas_call(kernel, out_shape=out, name=name, in_specs=[pl.BlockSpec(m...  6.67 us
  transfers between devices with their start and end apart: 1, of which 1 were waited for; matrix products, arithmetic and copies ran while one was open for 0% of the time, Pallas kernels for 0%

profile of v6, /device:TPU:1, one launch (start us, length us, event | category | flops | bytes accessed | tf_op | source)
XLA Modules:
  0.0 72.8 jit_solution(8839425507881197085)
XLA Ops:
  0.6 1.8 %first.1 = (f32[8,1024]{1,0:T(8,128)S(1)}, f32[8,1024]{1,0:T(8,128)S(1)}, f32[256,128]{1,0:T(8,128)S(1)}, f32[8,1024]{1,0:T(8,128)S(1)}, f32[2,8,128]{2,1,0:T(8,...) custom-call(f32[7,1024]{1,0:T(8,128)} %rhs_hbm.1, ...), custom_call_target="tpu_custom_call" | custom-call | tf_op jit(solution)/shard_map/first/pallas_call | solution.py:370
  2.5 12.7 %all_to_all.51 = f32[32,8,128]{2,1,0:T(8,128)S(1)} all-to-all(f32[32,8,128]{2,1,0:T(8,128)S(1)} %bitcast.577), channel_id=1, replica_groups={{168,160,184,176,136,128,152,144,232,224,248,240,200,192,216,208,40,32,..., dimensions={0} | all-to-all | bytes 262144 | tf_op jit(solution)/shard_map/all_to_all | solution.py:417
  15.2 1.0 %step.3 = (f32[8,1024]{1,0:T(8,128)S(1)}, f32[8,1024]{1,0:T(8,128)S(1)}, f32[256,128]{1,0:T(8,128)S(1)}, f32[8,1024]{1,0:T(8,128)S(1)}, f32[2,8,128]{2,1,0:T(8,128)S(1)}) custom-call(f32[256,128]{1,0:T(8,128)S(1)} %bitcast.571, s32[1,32,128]{2,1,0:T(8,128)S(1)} %get-tuple-element.176.cells_ref, f32[8,1024]{1,0:T(8,128)S(1)} %get-tuple-element.177.y_ref, ...), custom_call_target="tpu_custom_call" | custom-call | tf_op jit(solution)/shard_map/step/pallas_call | solution.py:370
  16.1 10.7 %all_to_all.52 = f32[32,8,128]{2,1,0:T(8,128)S(1)} all-to-all(f32[32,8,128]{2,1,0:T(8,128)S(1)} %bitcast.578), channel_id=1, replica_groups={{168,160,184,176,136,128,152,144,232,224,248,240,200,192,216,208,40,32,..., dimensions={0} | all-to-all | bytes 262144 | tf_op jit(solution)/shard_map/all_to_all | solution.py:417
  26.8 1.0 %step.4 = (f32[8,1024]{1,0:T(8,128)S(1)}, f32[8,1024]{1,0:T(8,128)S(1)}, f32[256,128]{1,0:T(8,128)S(1)}, f32[8,1024]{1,0:T(8,128)S(1)}, f32[2,8,128]{2,1,0:T(8,128)S(1)}) custom-call(f32[256,128]{1,0:T(8,128)S(1)} %bitcast.572, s32[1,32,128]{2,1,0:T(8,128)S(1)} %get-tuple-element.176.cells_ref, f32[8,1024]{1,0:T(8,128)S(1)} %get-tuple-element.187.y_ref, ...), custom_call_target="tpu_custom_call" | custom-call | tf_op jit(solution)/shard_map/step/pallas_call | solution.py:370
  27.8 0.0 copy-start.5
  27.8 0.0 copy-start.6
  27.8 0.0 copy-start.7
  27.8 0.0 copy-start.8
  27.9 0.0 copy-start.14
  27.9 0.0 copy-start.15
  27.9 0.0 copy-start.16
  27.9 0.0 copy-start.38
  27.9 10.8 %all_to_all.53 = f32[32,8,128]{2,1,0:T(8,128)S(1)} all-to-all(f32[32,8,128]{2,1,0:T(8,128)S(1)} %bitcast.579), channel_id=1, replica_groups={{168,160,184,176,136,128,152,144,232,224,248,240,200,192,216,208,40,32,..., dimensions={0} | all-to-all | bytes 262144 | tf_op jit(solution)/shard_map/all_to_all | solution.py:417
  38.7 1.0 %step.5 = (f32[8,1024]{1,0:T(8,128)S(1)}, f32[8,1024]{1,0:T(8,128)S(1)}, f32[256,128]{1,0:T(8,128)S(1)}, f32[8,1024]{1,0:T(8,128)S(1)}, f32[2,8,128]{2,1,0:T(8,128)S(1)}) custom-call(f32[256,128]{1,0:T(8,128)S(1)} %bitcast.570, s32[1,32,128]{2,1,0:T(8,128)S(1)} %get-tuple-element.176.cells_ref, f32[8,1024]{1,0:T(8,128)S(1)} %get-tuple-element.190.y_ref, ...), custom_call_target="tpu_custom_call" | custom-call | tf_op jit(solution)/shard_map/step/pallas_call | solution.py:370
  39.7 10.7 %all_to_all.54 = f32[32,8,128]{2,1,0:T(8,128)S(1)} all-to-all(f32[32,8,128]{2,1,0:T(8,128)S(1)} %bitcast.576), channel_id=1, replica_groups={{168,160,184,176,136,128,152,144,232,224,248,240,200,192,216,208,40,32,..., dimensions={0} | all-to-all | bytes 262144 | tf_op jit(solution)/shard_map/all_to_all | solution.py:417
  50.4 0.7 last.1
  51.2 0.5 collective-permute-start
  51.6 0.8 %collective-permute-done.other_ref = f32[8,128]{1,0:T(8,128)S(1)} collective-permute-done((f32[8,128]{1,0:T(8,128)S(1)}, f32[8,128]{1,0:T(8,128)S(1)}, u32[]{:S(2)}, u32[]{:S(2)}) %collective-permute-start) | collective-permute-done | bytes 4128 | tf_op jit(solution)/shard_map/ppermute | solution.py:431
  52.4 0.1 pair.1
  52.5 18.7 %all_to_all.55 = f32[128,1,128]{2,1,0:T(1,128)S(1)} all-to-all(f32[128,1,128]{2,1,0:T(1,128)S(1)} %bitcast.574), channel_id=1, replica_groups={{164,0,1,7,16,48,64,192,2,6,17,23,32,49,55,65,71,80,112,128,193,199,208..., dimensions={0} | all-to-all | bytes 131072 | tf_op jit(solution)/shard_map/all_to_all | solution.py:434
  71.2 1.1 %finish.1 = (f32[7,1024]{1,0:T(8,128)}, f32[7,1024]{1,0:T(8,128)}, s32[1,128]{1,0:T(1,128)S(1)}) custom-call(f32[128,128]{1,0:T(8,128)S(1)} %bitcast.575, f32[8,1024]{1,0:T(8,128)S(1)} %get-tuple-element.185.refs_0_, f32[8,1024]{1,0:T(8,128)S(1)} %get-tuple-element.188.refs_1_, f32[8,1024]{1,0:T(8,128)S(1)} %get-tuple-element.191.refs_2_, ...), custom_call_target="tpu_custom_call" | custom-call | tf_op jit(solution)/shard_map/finish/pallas_call | solution.py:370
  72.3 0.0 copy-done.5
  72.3 0.0 copy-done.6
  72.4 0.0 copy-done.7
  72.4 0.0 copy-done.8
  72.4 0.0 copy-done.14
  72.4 0.0 copy-done.15
  72.4 0.0 copy-done.16
  72.4 0.0 copy-done.38
  72.4 0.2 conditional.1
Async XLA Ops:
  27.8 44.5 %copy-start.5 = (f32[1,7,7,32,128]{4,3,2,1,0:T(8,128)S(1)}, f32[1,7,7,32,128]{4,3,2,1,0:T(8,128)}, u32[]{:S(2)}) copy-start(f32[1,7,7,32,128]{4,3,2,1,0:T(8,128)} %coup_hbm.1) | copy-start | bytes 2408452
  27.8 44.5 %copy-start.6 = (f32[7,7,1024]{2,1,0:T(8,128)S(1)}, f32[7,7,1024]{2,1,0:T(8,128)}, u32[]{:S(2)}) copy-start(f32[7,7,1024]{2,1,0:T(8,128)} %pre_hbm.1) | copy-start | bytes 602116
  27.8 44.5 %copy-start.7 = (f32[7,7,1024]{2,1,0:T(8,128)S(1)}, f32[7,7,1024]{2,1,0:T(8,128)}, u32[]{:S(2)}) copy-start(f32[7,7,1024]{2,1,0:T(8,128)} %diag_hbm.1) | copy-start | bytes 602116
  27.8 44.5 %copy-start.8 = (f32[7,7,1024]{2,1,0:T(8,128)S(1)}, f32[7,7,1024]{2,1,0:T(8,128)}, u32[]{:S(2)}) copy-start(f32[7,7,1024]{2,1,0:T(8,128)} %low_hbm.1) | copy-start | bytes 602116
  27.9 44.5 %copy-start.14 = (s32[1,32,128]{2,1,0:T(8,128)S(1)}, s32[1,32,128]{2,1,0:T(8,128)}, u32[]{:S(2)}) copy-start(s32[1,32,128]{2,1,0:T(8,128)} %send_hbm.1) | copy-start | bytes 49156
  27.9 44.5 %copy-start.15 = (f32[7,1024]{1,0:T(8,128)S(1)}, f32[7,1024]{1,0:T(8,128)}, u32[]{:S(2)}) copy-start(f32[7,1024]{1,0:T(8,128)} %rhs_hbm.1) | copy-start | bytes 86020
  27.9 44.5 %copy-start.16 = (s32[1,32,128]{2,1,0:T(8,128)S(1)}, s32[1,32,128]{2,1,0:T(8,128)}, u32[]{:S(2)}) copy-start(s32[1,32,128]{2,1,0:T(8,128)} %cells_hbm.1) | copy-start | bytes 49156
  27.9 44.5 %copy-start.38 = (s32[1,32]{1,0:T(1,128)S(1)}, s32[1,32]{1,0:T(1,128)}, u32[]{:S(2)}) copy-start(s32[1,32]{1,0:T(1,128)} %halo_hbm.1) | copy-start | bytes 388
  51.2 1.3 %collective-permute-start = (f32[8,128]{1,0:T(8,128)S(1)}, f32[8,128]{1,0:T(8,128)S(1)}, u32[]{:S(2)}, u32[]{:S(2)}) collective-permute-start(f32[8,128]{1,0:T(8,128)S(1)} %get-tuple-element.199.own_ref), channel_id=1, source_target_pairs={{0,8},{8,0},{16,24},{24,16},{32,40},{40,32},{48,56},{56,48},{64,72... | collective-permute-start | bytes 12296 | tf_op jit(solution)/shard_map/ppermute | solution.py:431

commit v7 on v4

--- a/solution.py
+++ b/solution.py
@@ -107,6 +107,16 @@
     return quick_sum(q, rest[0] * inverse)
 
 
+def turns(blk):
+    side = math.isqrt(blk // 2)
+    return side // 2, side // 2 * 2 + 1
+
+
+def place_of(peer, blk):
+    y, turn = turns(blk)
+    return (y - peer // 8) % (blk // 8) * 8 + (peer - turn) % 8
+
+
 def row_sums(parts):
     rows = [jnp.sum(part, axis=0, keepdims=True) for part in parts]
     return jnp.concatenate(rows + [jnp.zeros_like(rows[0])], axis=0)
@@ -140,6 +150,7 @@
 
 def mix(taken, coup_ref, halo_ref, msg_ref):
     peers = halo_ref.shape[1]
+    turn = turns(peers)[1]
     lanes = lax.broadcasted_iota(jnp.int32, (8, LANES), 1)
     rows = lax.broadcasted_iota(jnp.int32, (8, peers), 0)
     cols = lax.broadcasted_iota(jnp.int32, (8, peers), 1)
@@ -147,11 +158,12 @@
     for q in range(peers // 8):
         size = jnp.sum(jnp.where(cols == rows + q * 8, lens, 0), axis=1, keepdims=True)
         live = lanes < size
+        place = place_of(q * 8, peers) // 8 * 8
         for i in range(F):
             total = coup_ref[0, i, 0, q * 8 : (q + 1) * 8, :] * taken[q][0]
             for j in range(1, F):
                 total = total + coup_ref[0, i, j, q * 8 : (q + 1) * 8, :] * taken[q][j]
-            msg_ref[pl.ds(q * 64 + i, 8, stride=8), :] = jnp.where(live, total, 0.0)
+            msg_ref[pl.ds(place * 8 + i, 8, stride=8), :] = pltpu.roll(jnp.where(live, total, 0.0), 8 - turn, 0)
         msg_ref[pl.ds(q * 64 + F, 8, stride=8), :] = jnp.zeros((8, LANES), jnp.float32)
 
 
@@ -160,7 +172,8 @@
     spots = lax.broadcasted_iota(jnp.int32, (LANES, LANES), 0)
     left, right = [], []
     for s in range(peers):
-        x = recv_ref[s * 8 : (s + 1) * 8, :]
+        place = place_of(s, peers)
+        x = recv_ref[place * 8 : (place + 1) * 8, :]
         first = x.astype(jnp.bfloat16).astype(jnp.float32)
         second = x - first
         cell = cells_ref[0, s : s + 1, :]
@@ -396,8 +409,10 @@
     )
     face, blocks, recv_cells = kept[:4], kept[4:7], kept[7]
     us, zs, grams = [u], [z], [gram]
+    order = sorted(range(peers), key=lambda peer: place_of(peer, peers))
     for col in range(ITERS):
-        got = lax.all_to_all(msg.reshape(peers, 8, LANES), "blk", 0, 0, tiled=True).reshape(peers * 8, LANES)
+        got = lax.all_to_all(msg.reshape(peers, 8, LANES), "blk", 0, 0, axis_index_groups=[order], tiled=True)
+        got = got.reshape(peers * 8, LANES)
         if col < ITERS - 1:
             u, z, msg, y, gram = call(
                 functools.partial(step_kernel, col + 1),

time: 77.5 us -> 72.3 us (0.933)
  blocking collectives: 67.9 us -> 62.7 us
    all_to_all x4, blocking collectives: 50 us -> 44.4 us  [per_device(): lax.all_to_all(msg.reshape(peers, 8, LANES), 'blk', 0, 0, axis_index_grou...]
where the time goes in v7:
time: 72.3 us; the launch traced here: 71.9 us
  blocking collectives  62.7 us (87%)
  Pallas kernels  6.64 us (9%)
  between operations  1.01 us (1%)
  waiting for transfers between devices  0.82 us (1%)
    all_to_all x4, blocking collectives, per_device(): lax.all_to_all(msg.reshape(peers, 8, LANES), 'blk', 0, 0, axis_index_grou...  44.4 us
    all_to_all x1, blocking collectives, per_device(): got = lax.all_to_all(msg, BOTH, 0, 0, axis_index_groups=groups, tiled=True)  18.3 us
    pallas_call x7, Pallas kernels, call(): pl.pallas_call(kernel, out_shape=out, name=name, in_specs=[pl.BlockSpec(m...  6.64 us
  transfers between devices with their start and end apart: 1, of which 1 were waited for; matrix products, arithmetic and copies ran while one was open for 0% of the time, Pallas kernels for 0%

profile of v7, /device:TPU:1, one launch (start us, length us, event | category | flops | bytes accessed | tf_op | source)
XLA Modules:
  0.0 71.9 jit_solution(16157838346613524205)
XLA Ops:
  0.6 1.8 %first.1 = (f32[8,1024]{1,0:T(8,128)S(1)}, f32[8,1024]{1,0:T(8,128)S(1)}, f32[256,128]{1,0:T(8,128)S(1)}, f32[8,1024]{1,0:T(8,128)S(1)}, f32[2,8,128]{2,1,0:T(8,...) custom-call(f32[7,1024]{1,0:T(8,128)} %rhs_hbm.1, ...), custom_call_target="tpu_custom_call" | custom-call | tf_op jit(solution)/shard_map/first/pallas_call | solution.py:367
  2.5 12.7 %all_to_all.51 = f32[32,8,128]{2,1,0:T(8,128)S(1)} all-to-all(f32[32,8,128]{2,1,0:T(8,128)S(1)} %bitcast.577), channel_id=1, replica_groups={{168,176,184,128,136,144,152,160,104,112,120,64,72,80,88,96,40,48,56,0,..., dimensions={0} | all-to-all | bytes 262144 | tf_op jit(solution)/shard_map/all_to_all | solution.py:414
  15.2 1.0 %step.3 = (f32[8,1024]{1,0:T(8,128)S(1)}, f32[8,1024]{1,0:T(8,128)S(1)}, f32[256,128]{1,0:T(8,128)S(1)}, f32[8,1024]{1,0:T(8,128)S(1)}, f32[2,8,128]{2,1,0:T(8,128)S(1)}) custom-call(f32[256,128]{1,0:T(8,128)S(1)} %bitcast.571, s32[1,32,128]{2,1,0:T(8,128)S(1)} %get-tuple-element.176.cells_ref, f32[8,1024]{1,0:T(8,128)S(1)} %get-tuple-element.177.y_ref, ...), custom_call_target="tpu_custom_call" | custom-call | tf_op jit(solution)/shard_map/step/pallas_call | solution.py:367
  16.2 10.5 %all_to_all.52 = f32[32,8,128]{2,1,0:T(8,128)S(1)} all-to-all(f32[32,8,128]{2,1,0:T(8,128)S(1)} %bitcast.578), channel_id=1, replica_groups={{168,176,184,128,136,144,152,160,104,112,120,64,72,80,88,96,40,48,56,0,..., dimensions={0} | all-to-all | bytes 262144 | tf_op jit(solution)/shard_map/all_to_all | solution.py:414
  26.7 1.0 %step.4 = (f32[8,1024]{1,0:T(8,128)S(1)}, f32[8,1024]{1,0:T(8,128)S(1)}, f32[256,128]{1,0:T(8,128)S(1)}, f32[8,1024]{1,0:T(8,128)S(1)}, f32[2,8,128]{2,1,0:T(8,128)S(1)}) custom-call(f32[256,128]{1,0:T(8,128)S(1)} %bitcast.572, s32[1,32,128]{2,1,0:T(8,128)S(1)} %get-tuple-element.176.cells_ref, f32[8,1024]{1,0:T(8,128)S(1)} %get-tuple-element.187.y_ref, ...), custom_call_target="tpu_custom_call" | custom-call | tf_op jit(solution)/shard_map/step/pallas_call | solution.py:367
  27.6 0.0 copy-start.5
  27.7 0.0 copy-start.6
  27.7 0.0 copy-start.7
  27.7 0.0 copy-start.8
  27.7 0.0 copy-start.14
  27.7 0.0 copy-start.15
  27.7 0.0 copy-start.16
  27.7 0.0 copy-start.38
  27.7 10.6 %all_to_all.53 = f32[32,8,128]{2,1,0:T(8,128)S(1)} all-to-all(f32[32,8,128]{2,1,0:T(8,128)S(1)} %bitcast.579), channel_id=1, replica_groups={{168,176,184,128,136,144,152,160,104,112,120,64,72,80,88,96,40,48,56,0,..., dimensions={0} | all-to-all | bytes 262144 | tf_op jit(solution)/shard_map/all_to_all | solution.py:414
  38.4 1.0 %step.5 = (f32[8,1024]{1,0:T(8,128)S(1)}, f32[8,1024]{1,0:T(8,128)S(1)}, f32[256,128]{1,0:T(8,128)S(1)}, f32[8,1024]{1,0:T(8,128)S(1)}, f32[2,8,128]{2,1,0:T(8,128)S(1)}) custom-call(f32[256,128]{1,0:T(8,128)S(1)} %bitcast.570, s32[1,32,128]{2,1,0:T(8,128)S(1)} %get-tuple-element.176.cells_ref, f32[8,1024]{1,0:T(8,128)S(1)} %get-tuple-element.190.y_ref, ...), custom_call_target="tpu_custom_call" | custom-call | tf_op jit(solution)/shard_map/step/pallas_call | solution.py:367
  39.4 10.5 %all_to_all.54 = f32[32,8,128]{2,1,0:T(8,128)S(1)} all-to-all(f32[32,8,128]{2,1,0:T(8,128)S(1)} %bitcast.576), channel_id=1, replica_groups={{168,176,184,128,136,144,152,160,104,112,120,64,72,80,88,96,40,48,56,0,..., dimensions={0} | all-to-all | bytes 262144 | tf_op jit(solution)/shard_map/all_to_all | solution.py:414
  49.9 0.7 last.1
  50.6 0.4 collective-permute-start
  51.1 0.8 %collective-permute-done.other_ref = f32[8,128]{1,0:T(8,128)S(1)} collective-permute-done((f32[8,128]{1,0:T(8,128)S(1)}, f32[8,128]{1,0:T(8,128)S(1)}, u32[]{:S(2)}, u32[]{:S(2)}) %collective-permute-start) | collective-permute-done | bytes 4128 | tf_op jit(solution)/shard_map/ppermute | solution.py:428
  51.9 0.1 pair.1
  52.0 18.3 %all_to_all.55 = f32[128,1,128]{2,1,0:T(1,128)S(1)} all-to-all(f32[128,1,128]{2,1,0:T(1,128)S(1)} %bitcast.574), channel_id=1, replica_groups={{164,0,1,7,16,48,64,192,2,6,17,23,32,49,55,65,71,80,112,128,193,199,208..., dimensions={0} | all-to-all | bytes 131072 | tf_op jit(solution)/shard_map/all_to_all | solution.py:431
  70.3 1.1 %finish.1 = (f32[7,1024]{1,0:T(8,128)}, f32[7,1024]{1,0:T(8,128)}, s32[1,128]{1,0:T(1,128)S(1)}) custom-call(f32[128,128]{1,0:T(8,128)S(1)} %bitcast.575, f32[8,1024]{1,0:T(8,128)S(1)} %get-tuple-element.185.refs_0_, f32[8,1024]{1,0:T(8,128)S(1)} %get-tuple-element.188.refs_1_, f32[8,1024]{1,0:T(8,128)S(1)} %get-tuple-element.191.refs_2_, ...), custom_call_target="tpu_custom_call" | custom-call | tf_op jit(solution)/shard_map/finish/pallas_call | solution.py:367
  71.4 0.0 copy-done.5
  71.4 0.0 copy-done.6
  71.4 0.0 copy-done.7
  71.4 0.0 copy-done.8
  71.5 0.0 copy-done.14
  71.5 0.0 copy-done.15
  71.5 0.0 copy-done.16
  71.5 0.0 copy-done.38
  71.5 0.2 conditional.1
Async XLA Ops:
  27.6 43.8 %copy-start.5 = (f32[1,7,7,32,128]{4,3,2,1,0:T(8,128)S(1)}, f32[1,7,7,32,128]{4,3,2,1,0:T(8,128)}, u32[]{:S(2)}) copy-start(f32[1,7,7,32,128]{4,3,2,1,0:T(8,128)} %coup_hbm.1) | copy-start | bytes 2408452
  27.7 43.8 %copy-start.6 = (f32[7,7,1024]{2,1,0:T(8,128)S(1)}, f32[7,7,1024]{2,1,0:T(8,128)}, u32[]{:S(2)}) copy-start(f32[7,7,1024]{2,1,0:T(8,128)} %pre_hbm.1) | copy-start | bytes 602116
  27.7 43.8 %copy-start.7 = (f32[7,7,1024]{2,1,0:T(8,128)S(1)}, f32[7,7,1024]{2,1,0:T(8,128)}, u32[]{:S(2)}) copy-start(f32[7,7,1024]{2,1,0:T(8,128)} %diag_hbm.1) | copy-start | bytes 602116
  27.7 43.8 %copy-start.8 = (f32[7,7,1024]{2,1,0:T(8,128)S(1)}, f32[7,7,1024]{2,1,0:T(8,128)}, u32[]{:S(2)}) copy-start(f32[7,7,1024]{2,1,0:T(8,128)} %low_hbm.1) | copy-start | bytes 602116
  27.7 43.8 %copy-start.14 = (s32[1,32,128]{2,1,0:T(8,128)S(1)}, s32[1,32,128]{2,1,0:T(8,128)}, u32[]{:S(2)}) copy-start(s32[1,32,128]{2,1,0:T(8,128)} %send_hbm.1) | copy-start | bytes 49156
  27.7 43.8 %copy-start.15 = (f32[7,1024]{1,0:T(8,128)S(1)}, f32[7,1024]{1,0:T(8,128)}, u32[]{:S(2)}) copy-start(f32[7,1024]{1,0:T(8,128)} %rhs_hbm.1) | copy-start | bytes 86020
  27.7 43.8 %copy-start.16 = (s32[1,32,128]{2,1,0:T(8,128)S(1)}, s32[1,32,128]{2,1,0:T(8,128)}, u32[]{:S(2)}) copy-start(s32[1,32,128]{2,1,0:T(8,128)} %cells_hbm.1) | copy-start | bytes 49156
  27.7 43.8 %copy-start.38 = (s32[1,32]{1,0:T(1,128)S(1)}, s32[1,32]{1,0:T(1,128)}, u32[]{:S(2)}) copy-start(s32[1,32]{1,0:T(1,128)} %halo_hbm.1) | copy-start | bytes 388
  50.6 1.3 %collective-permute-start = (f32[8,128]{1,0:T(8,128)S(1)}, f32[8,128]{1,0:T(8,128)S(1)}, u32[]{:S(2)}, u32[]{:S(2)}) collective-permute-start(f32[8,128]{1,0:T(8,128)S(1)} %get-tuple-element.199.own_ref), channel_id=1, source_target_pairs={{0,8},{8,0},{16,24},{24,16},{32,40},{40,32},{48,56},{56,48},{64,72... | collective-permute-start | bytes 12296 | tf_op jit(solution)/shard_map/ppermute | solution.py:428

commit v8 on v7

--- a/solution.py
+++ b/solution.py
@@ -292,7 +292,9 @@
 
 
 def pair_kernel(own_ref, other_ref, msg_ref):
-    total, error = two_sum(own_ref[...], other_ref[...])
+    own, other = own_ref[...], other_ref[...]
+    ahead = jnp.abs(own) >= jnp.abs(other)
+    total, error = quick_sum(jnp.where(ahead, own, other), jnp.where(ahead, other, own))
     lane = lax.broadcasted_iota(jnp.int32, total.shape, 1)
     row = jnp.where(lane < 64, total, total + pltpu.roll(error, 64, 1))
     msg_ref[...] = jnp.concatenate([row] * (msg_ref.shape[0] // 8), axis=0)

time: 72.3 us -> 72.3 us (level)
  no operation moved by 1% of the time
where the time goes in v8:
time: 72.3 us; the launch traced here: 71.9 us
  blocking collectives  62.7 us (87%)
  Pallas kernels  6.64 us (9%)
  between operations  1.01 us (1%)
  waiting for transfers between devices  0.82 us (1%)
    all_to_all x4, blocking collectives, per_device(): lax.all_to_all(msg.reshape(peers, 8, LANES), 'blk', 0, 0, axis_index_grou...  44.4 us
    all_to_all x1, blocking collectives, per_device(): got = lax.all_to_all(msg, BOTH, 0, 0, axis_index_groups=groups, tiled=True)  18.3 us
    pallas_call x7, Pallas kernels, call(): pl.pallas_call(kernel, out_shape=out, name=name, in_specs=[pl.BlockSpec(m...  6.64 us
  transfers between devices with their start and end apart: 1, of which 1 were waited for; matrix products, arithmetic and copies ran while one was open for 0% of the time, Pallas kernels for 0%

profile of v8, /device:TPU:1, one launch (start us, length us, event | category | flops | bytes accessed | tf_op | source)
XLA Modules:
  0.0 71.9 jit_solution(7868989838338123212)
XLA Ops:
  0.6 1.8 %first.1 = (f32[8,1024]{1,0:T(8,128)S(1)}, f32[8,1024]{1,0:T(8,128)S(1)}, f32[256,128]{1,0:T(8,128)S(1)}, f32[8,1024]{1,0:T(8,128)S(1)}, f32[2,8,128]{2,1,0:T(8,...) custom-call(f32[7,1024]{1,0:T(8,128)} %rhs_hbm.1, ...), custom_call_target="tpu_custom_call" | custom-call | tf_op jit(solution)/shard_map/first/pallas_call | solution.py:369
  2.5 12.7 %all_to_all.51 = f32[32,8,128]{2,1,0:T(8,128)S(1)} all-to-all(f32[32,8,128]{2,1,0:T(8,128)S(1)} %bitcast.577), channel_id=1, replica_groups={{168,176,184,128,136,144,152,160,104,112,120,64,72,80,88,96,40,48,56,0,..., dimensions={0} | all-to-all | bytes 262144 | tf_op jit(solution)/shard_map/all_to_all | solution.py:416
  15.2 1.0 %step.3 = (f32[8,1024]{1,0:T(8,128)S(1)}, f32[8,1024]{1,0:T(8,128)S(1)}, f32[256,128]{1,0:T(8,128)S(1)}, f32[8,1024]{1,0:T(8,128)S(1)}, f32[2,8,128]{2,1,0:T(8,128)S(1)}) custom-call(f32[256,128]{1,0:T(8,128)S(1)} %bitcast.571, s32[1,32,128]{2,1,0:T(8,128)S(1)} %get-tuple-element.176.cells_ref, f32[8,1024]{1,0:T(8,128)S(1)} %get-tuple-element.177.y_ref, ...), custom_call_target="tpu_custom_call" | custom-call | tf_op jit(solution)/shard_map/step/pallas_call | solution.py:369
  16.2 10.5 %all_to_all.52 = f32[32,8,128]{2,1,0:T(8,128)S(1)} all-to-all(f32[32,8,128]{2,1,0:T(8,128)S(1)} %bitcast.578), channel_id=1, replica_groups={{168,176,184,128,136,144,152,160,104,112,120,64,72,80,88,96,40,48,56,0,..., dimensions={0} | all-to-all | bytes 262144 | tf_op jit(solution)/shard_map/all_to_all | solution.py:416
  26.7 1.0 %step.4 = (f32[8,1024]{1,0:T(8,128)S(1)}, f32[8,1024]{1,0:T(8,128)S(1)}, f32[256,128]{1,0:T(8,128)S(1)}, f32[8,1024]{1,0:T(8,128)S(1)}, f32[2,8,128]{2,1,0:T(8,128)S(1)}) custom-call(f32[256,128]{1,0:T(8,128)S(1)} %bitcast.572, s32[1,32,128]{2,1,0:T(8,128)S(1)} %get-tuple-element.176.cells_ref, f32[8,1024]{1,0:T(8,128)S(1)} %get-tuple-element.187.y_ref, ...), custom_call_target="tpu_custom_call" | custom-call | tf_op jit(solution)/shard_map/step/pallas_call | solution.py:369
  27.6 0.0 copy-start.5
  27.7 0.0 copy-start.6
  27.7 0.0 copy-start.7
  27.7 0.0 copy-start.8
  27.7 0.0 copy-start.14
  27.7 0.0 copy-start.15
  27.7 0.0 copy-start.16
  27.7 0.0 copy-start.38
  27.7 10.6 %all_to_all.53 = f32[32,8,128]{2,1,0:T(8,128)S(1)} all-to-all(f32[32,8,128]{2,1,0:T(8,128)S(1)} %bitcast.579), channel_id=1, replica_groups={{168,176,184,128,136,144,152,160,104,112,120,64,72,80,88,96,40,48,56,0,..., dimensions={0} | all-to-all | bytes 262144 | tf_op jit(solution)/shard_map/all_to_all | solution.py:416
  38.4 1.0 %step.5 = (f32[8,1024]{1,0:T(8,128)S(1)}, f32[8,1024]{1,0:T(8,128)S(1)}, f32[256,128]{1,0:T(8,128)S(1)}, f32[8,1024]{1,0:T(8,128)S(1)}, f32[2,8,128]{2,1,0:T(8,128)S(1)}) custom-call(f32[256,128]{1,0:T(8,128)S(1)} %bitcast.570, s32[1,32,128]{2,1,0:T(8,128)S(1)} %get-tuple-element.176.cells_ref, f32[8,1024]{1,0:T(8,128)S(1)} %get-tuple-element.190.y_ref, ...), custom_call_target="tpu_custom_call" | custom-call | tf_op jit(solution)/shard_map/step/pallas_call | solution.py:369
  39.4 10.5 %all_to_all.54 = f32[32,8,128]{2,1,0:T(8,128)S(1)} all-to-all(f32[32,8,128]{2,1,0:T(8,128)S(1)} %bitcast.576), channel_id=1, replica_groups={{168,176,184,128,136,144,152,160,104,112,120,64,72,80,88,96,40,48,56,0,..., dimensions={0} | all-to-all | bytes 262144 | tf_op jit(solution)/shard_map/all_to_all | solution.py:416
  49.9 0.7 last.1
  50.6 0.4 collective-permute-start
  51.1 0.8 %collective-permute-done.other_ref = f32[8,128]{1,0:T(8,128)S(1)} collective-permute-done((f32[8,128]{1,0:T(8,128)S(1)}, f32[8,128]{1,0:T(8,128)S(1)}, u32[]{:S(2)}, u32[]{:S(2)}) %collective-permute-start) | collective-permute-done | bytes 4128 | tf_op jit(solution)/shard_map/ppermute | solution.py:430
  51.9 0.1 pair.1
  52.0 18.3 %all_to_all.55 = f32[128,1,128]{2,1,0:T(1,128)S(1)} all-to-all(f32[128,1,128]{2,1,0:T(1,128)S(1)} %bitcast.574), channel_id=1, replica_groups={{164,0,1,7,16,48,64,192,2,6,17,23,32,49,55,65,71,80,112,128,193,199,208..., dimensions={0} | all-to-all | bytes 131072 | tf_op jit(solution)/shard_map/all_to_all | solution.py:433
  70.3 1.1 %finish.1 = (f32[7,1024]{1,0:T(8,128)}, f32[7,1024]{1,0:T(8,128)}, s32[1,128]{1,0:T(1,128)S(1)}) custom-call(f32[128,128]{1,0:T(8,128)S(1)} %bitcast.575, f32[8,1024]{1,0:T(8,128)S(1)} %get-tuple-element.185.refs_0_, f32[8,1024]{1,0:T(8,128)S(1)} %get-tuple-element.188.refs_1_, f32[8,1024]{1,0:T(8,128)S(1)} %get-tuple-element.191.refs_2_, ...), custom_call_target="tpu_custom_call" | custom-call | tf_op jit(solution)/shard_map/finish/pallas_call | solution.py:369
  71.4 0.0 copy-done.5
  71.4 0.0 copy-done.6
  71.4 0.0 copy-done.7
  71.4 0.0 copy-done.8
  71.5 0.0 copy-done.14
  71.5 0.0 copy-done.15
  71.5 0.0 copy-done.16
  71.5 0.0 copy-done.38
  71.5 0.2 conditional.1
Async XLA Ops:
  27.6 43.8 %copy-start.5 = (f32[1,7,7,32,128]{4,3,2,1,0:T(8,128)S(1)}, f32[1,7,7,32,128]{4,3,2,1,0:T(8,128)}, u32[]{:S(2)}) copy-start(f32[1,7,7,32,128]{4,3,2,1,0:T(8,128)} %coup_hbm.1) | copy-start | bytes 2408452
  27.7 43.8 %copy-start.6 = (f32[7,7,1024]{2,1,0:T(8,128)S(1)}, f32[7,7,1024]{2,1,0:T(8,128)}, u32[]{:S(2)}) copy-start(f32[7,7,1024]{2,1,0:T(8,128)} %pre_hbm.1) | copy-start | bytes 602116
  27.7 43.8 %copy-start.7 = (f32[7,7,1024]{2,1,0:T(8,128)S(1)}, f32[7,7,1024]{2,1,0:T(8,128)}, u32[]{:S(2)}) copy-start(f32[7,7,1024]{2,1,0:T(8,128)} %diag_hbm.1) | copy-start | bytes 602116
  27.7 43.8 %copy-start.8 = (f32[7,7,1024]{2,1,0:T(8,128)S(1)}, f32[7,7,1024]{2,1,0:T(8,128)}, u32[]{:S(2)}) copy-start(f32[7,7,1024]{2,1,0:T(8,128)} %low_hbm.1) | copy-start | bytes 602116
  27.7 43.8 %copy-start.14 = (s32[1,32,128]{2,1,0:T(8,128)S(1)}, s32[1,32,128]{2,1,0:T(8,128)}, u32[]{:S(2)}) copy-start(s32[1,32,128]{2,1,0:T(8,128)} %send_hbm.1) | copy-start | bytes 49156
  27.7 43.8 %copy-start.15 = (f32[7,1024]{1,0:T(8,128)S(1)}, f32[7,1024]{1,0:T(8,128)}, u32[]{:S(2)}) copy-start(f32[7,1024]{1,0:T(8,128)} %rhs_hbm.1) | copy-start | bytes 86020
  27.7 43.8 %copy-start.16 = (s32[1,32,128]{2,1,0:T(8,128)S(1)}, s32[1,32,128]{2,1,0:T(8,128)}, u32[]{:S(2)}) copy-start(s32[1,32,128]{2,1,0:T(8,128)} %cells_hbm.1) | copy-start | bytes 49156
  27.7 43.8 %copy-start.38 = (s32[1,32]{1,0:T(1,128)S(1)}, s32[1,32]{1,0:T(1,128)}, u32[]{:S(2)}) copy-start(s32[1,32]{1,0:T(1,128)} %halo_hbm.1) | copy-start | bytes 388
  50.6 1.3 %collective-permute-start = (f32[8,128]{1,0:T(8,128)S(1)}, f32[8,128]{1,0:T(8,128)S(1)}, u32[]{:S(2)}, u32[]{:S(2)}) collective-permute-start(f32[8,128]{1,0:T(8,128)S(1)} %get-tuple-element.199.own_ref), channel_id=1, source_target_pairs={{0,8},{8,0},{16,24},{24,16},{32,40},{40,32},{48,56},{56,48},{64,72... | collective-permute-start | bytes 12296 | tf_op jit(solution)/shard_map/ppermute | solution.py:430

commit v9 on v8

--- a/solution.py
+++ b/solution.py
@@ -244,7 +244,7 @@
     rows = [(pre_hbm, pre_ref)]
     faces = [(coup_hbm, coup_ref)]
     blocks = [(diag_hbm, diag_ref), (low_hbm, low_ref), (up_hbm, up_ref), (cells_hbm, cells_ref)]
-    copies = [pltpu.make_async_copy(*pair, sems.at[k]) for k, pair in enumerate(whole + rows + faces + blocks)]
+    copies = [pltpu.make_async_copy(*pair, sems.at[k]) for k, pair in enumerate(whole + rows + blocks + faces)]
     for copy in copies:
         copy.start()
     for copy in copies[: len(whole)]:
@@ -257,12 +257,11 @@
     z = precondition(pre_ref, u)
     z_ref[...] = z
     taken = gather(z, send_ref)
-    for copy in copies[len(whole) + 1 : len(whole) + 2]:
-        copy.wait()
-    mix(taken, coup_ref, halo_ref, msg_ref)
-    for copy in copies[len(whole) + 2 :]:
+    for copy in copies[len(whole) + 1 : -1]:
         copy.wait()
     y_ref[...] = local_part(z, diag_ref, low_ref, up_ref)
+    copies[-1].wait()
+    mix(taken, coup_ref, halo_ref, msg_ref)
 
 
 def step_kernel(col, recv_ref, cells_ref, y_ref, pre_ref, coup_ref, send_ref, halo_ref, diag_ref, low_ref, up_ref, *refs):

time: 72.3 us -> 72.4 us (level)
  no operation moved by 1% of the time
where the time goes in v9:
time: 72.4 us; the launch traced here: 72 us
  blocking collectives  62.7 us (87%)
  Pallas kernels  6.71 us (9%)
  between operations  1.01 us (1%)
  waiting for transfers between devices  0.82 us (1%)
    all_to_all x4, blocking collectives, per_device(): lax.all_to_all(msg.reshape(peers, 8, LANES), 'blk', 0, 0, axis_index_grou...  44.4 us
    all_to_all x1, blocking collectives, per_device(): got = lax.all_to_all(msg, BOTH, 0, 0, axis_index_groups=groups, tiled=True)  18.3 us
    pallas_call x7, Pallas kernels, call(): pl.pallas_call(kernel, out_shape=out, name=name, in_specs=[pl.BlockSpec(m...  6.71 us
  transfers between devices with their start and end apart: 1, of which 1 were waited for; matrix products, arithmetic and copies ran while one was open for 0% of the time, Pallas kernels for 0%

profile of v9, /device:TPU:1, one launch (start us, length us, event | category | flops | bytes accessed | tf_op | source)
XLA Modules:
  0.0 72.0 jit_solution(16813564912227251940)
XLA Ops:
  0.6 1.9 %first.1 = (f32[8,1024]{1,0:T(8,128)S(1)}, f32[8,1024]{1,0:T(8,128)S(1)}, f32[256,128]{1,0:T(8,128)S(1)}, f32[8,1024]{1,0:T(8,128)S(1)}, f32[2,8,128]{2,1,0:T(8,...) custom-call(f32[7,1024]{1,0:T(8,128)} %rhs_hbm.1, ...), custom_call_target="tpu_custom_call" | custom-call | tf_op jit(solution)/shard_map/first/pallas_call | solution.py:368
  2.6 12.7 %all_to_all.51 = f32[32,8,128]{2,1,0:T(8,128)S(1)} all-to-all(f32[32,8,128]{2,1,0:T(8,128)S(1)} %bitcast.577), channel_id=1, replica_groups={{168,176,184,128,136,144,152,160,104,112,120,64,72,80,88,96,40,48,56,0,..., dimensions={0} | all-to-all | bytes 262144 | tf_op jit(solution)/shard_map/all_to_all | solution.py:415
  15.3 1.0 %step.3 = (f32[8,1024]{1,0:T(8,128)S(1)}, f32[8,1024]{1,0:T(8,128)S(1)}, f32[256,128]{1,0:T(8,128)S(1)}, f32[8,1024]{1,0:T(8,128)S(1)}, f32[2,8,128]{2,1,0:T(8,128)S(1)}) custom-call(f32[256,128]{1,0:T(8,128)S(1)} %bitcast.571, s32[1,32,128]{2,1,0:T(8,128)S(1)} %get-tuple-element.176.cells_ref, f32[8,1024]{1,0:T(8,128)S(1)} %get-tuple-element.177.y_ref, ...), custom_call_target="tpu_custom_call" | custom-call | tf_op jit(solution)/shard_map/step/pallas_call | solution.py:368
  16.2 10.5 %all_to_all.52 = f32[32,8,128]{2,1,0:T(8,128)S(1)} all-to-all(f32[32,8,128]{2,1,0:T(8,128)S(1)} %bitcast.578), channel_id=1, replica_groups={{168,176,184,128,136,144,152,160,104,112,120,64,72,80,88,96,40,48,56,0,..., dimensions={0} | all-to-all | bytes 262144 | tf_op jit(solution)/shard_map/all_to_all | solution.py:415
  26.7 1.0 %step.4 = (f32[8,1024]{1,0:T(8,128)S(1)}, f32[8,1024]{1,0:T(8,128)S(1)}, f32[256,128]{1,0:T(8,128)S(1)}, f32[8,1024]{1,0:T(8,128)S(1)}, f32[2,8,128]{2,1,0:T(8,128)S(1)}) custom-call(f32[256,128]{1,0:T(8,128)S(1)} %bitcast.572, s32[1,32,128]{2,1,0:T(8,128)S(1)} %get-tuple-element.176.cells_ref, f32[8,1024]{1,0:T(8,128)S(1)} %get-tuple-element.187.y_ref, ...), custom_call_target="tpu_custom_call" | custom-call | tf_op jit(solution)/shard_map/step/pallas_call | solution.py:368
  27.7 0.0 copy-start.5
  27.7 0.0 copy-start.6
  27.7 0.0 copy-start.7
  27.7 0.0 copy-start.8
  27.8 0.0 copy-start.14
  27.8 0.0 copy-start.15
  27.8 0.0 copy-start.16
  27.8 0.0 copy-start.38
  27.8 10.6 %all_to_all.53 = f32[32,8,128]{2,1,0:T(8,128)S(1)} all-to-all(f32[32,8,128]{2,1,0:T(8,128)S(1)} %bitcast.579), channel_id=1, replica_groups={{168,176,184,128,136,144,152,160,104,112,120,64,72,80,88,96,40,48,56,0,..., dimensions={0} | all-to-all | bytes 262144 | tf_op jit(solution)/shard_map/all_to_all | solution.py:415
  38.4 1.0 %step.5 = (f32[8,1024]{1,0:T(8,128)S(1)}, f32[8,1024]{1,0:T(8,128)S(1)}, f32[256,128]{1,0:T(8,128)S(1)}, f32[8,1024]{1,0:T(8,128)S(1)}, f32[2,8,128]{2,1,0:T(8,128)S(1)}) custom-call(f32[256,128]{1,0:T(8,128)S(1)} %bitcast.570, s32[1,32,128]{2,1,0:T(8,128)S(1)} %get-tuple-element.176.cells_ref, f32[8,1024]{1,0:T(8,128)S(1)} %get-tuple-element.190.y_ref, ...), custom_call_target="tpu_custom_call" | custom-call | tf_op jit(solution)/shard_map/step/pallas_call | solution.py:368
  39.5 10.5 %all_to_all.54 = f32[32,8,128]{2,1,0:T(8,128)S(1)} all-to-all(f32[32,8,128]{2,1,0:T(8,128)S(1)} %bitcast.576), channel_id=1, replica_groups={{168,176,184,128,136,144,152,160,104,112,120,64,72,80,88,96,40,48,56,0,..., dimensions={0} | all-to-all | bytes 262144 | tf_op jit(solution)/shard_map/all_to_all | solution.py:415
  50.0 0.7 last.1
  50.7 0.5 collective-permute-start
  51.1 0.8 %collective-permute-done.other_ref = f32[8,128]{1,0:T(8,128)S(1)} collective-permute-done((f32[8,128]{1,0:T(8,128)S(1)}, f32[8,128]{1,0:T(8,128)S(1)}, u32[]{:S(2)}, u32[]{:S(2)}) %collective-permute-start) | collective-permute-done | bytes 4128 | tf_op jit(solution)/shard_map/ppermute | solution.py:429
  51.9 0.1 pair.1
  52.0 18.3 %all_to_all.55 = f32[128,1,128]{2,1,0:T(1,128)S(1)} all-to-all(f32[128,1,128]{2,1,0:T(1,128)S(1)} %bitcast.574), channel_id=1, replica_groups={{164,0,1,7,16,48,64,192,2,6,17,23,32,49,55,65,71,80,112,128,193,199,208..., dimensions={0} | all-to-all | bytes 131072 | tf_op jit(solution)/shard_map/all_to_all | solution.py:432
  70.4 1.1 %finish.1 = (f32[7,1024]{1,0:T(8,128)}, f32[7,1024]{1,0:T(8,128)}, s32[1,128]{1,0:T(1,128)S(1)}) custom-call(f32[128,128]{1,0:T(8,128)S(1)} %bitcast.575, f32[8,1024]{1,0:T(8,128)S(1)} %get-tuple-element.185.refs_0_, f32[8,1024]{1,0:T(8,128)S(1)} %get-tuple-element.188.refs_1_, f32[8,1024]{1,0:T(8,128)S(1)} %get-tuple-element.191.refs_2_, ...), custom_call_target="tpu_custom_call" | custom-call | tf_op jit(solution)/shard_map/finish/pallas_call | solution.py:368
  71.5 0.0 copy-done.5
  71.5 0.0 copy-done.6
  71.5 0.0 copy-done.7
  71.5 0.0 copy-done.8
  71.5 0.0 copy-done.14
  71.5 0.0 copy-done.15
  71.6 0.0 copy-done.16
  71.6 0.0 copy-done.38
  71.6 0.2 conditional.1
Async XLA Ops:
  27.7 43.8 %copy-start.5 = (f32[1,7,7,32,128]{4,3,2,1,0:T(8,128)S(1)}, f32[1,7,7,32,128]{4,3,2,1,0:T(8,128)}, u32[]{:S(2)}) copy-start(f32[1,7,7,32,128]{4,3,2,1,0:T(8,128)} %coup_hbm.1) | copy-start | bytes 2408452
  27.7 43.8 %copy-start.6 = (f32[7,7,1024]{2,1,0:T(8,128)S(1)}, f32[7,7,1024]{2,1,0:T(8,128)}, u32[]{:S(2)}) copy-start(f32[7,7,1024]{2,1,0:T(8,128)} %pre_hbm.1) | copy-start | bytes 602116
  27.7 43.8 %copy-start.7 = (f32[7,7,1024]{2,1,0:T(8,128)S(1)}, f32[7,7,1024]{2,1,0:T(8,128)}, u32[]{:S(2)}) copy-start(f32[7,7,1024]{2,1,0:T(8,128)} %diag_hbm.1) | copy-start | bytes 602116
  27.7 43.8 %copy-start.8 = (f32[7,7,1024]{2,1,0:T(8,128)S(1)}, f32[7,7,1024]{2,1,0:T(8,128)}, u32[]{:S(2)}) copy-start(f32[7,7,1024]{2,1,0:T(8,128)} %low_hbm.1) | copy-start | bytes 602116
  27.8 43.8 %copy-start.14 = (s32[1,32,128]{2,1,0:T(8,128)S(1)}, s32[1,32,128]{2,1,0:T(8,128)}, u32[]{:S(2)}) copy-start(s32[1,32,128]{2,1,0:T(8,128)} %send_hbm.1) | copy-start | bytes 49156
  27.8 43.8 %copy-start.15 = (f32[7,1024]{1,0:T(8,128)S(1)}, f32[7,1024]{1,0:T(8,128)}, u32[]{:S(2)}) copy-start(f32[7,1024]{1,0:T(8,128)} %rhs_hbm.1) | copy-start | bytes 86020
  27.8 43.8 %copy-start.16 = (s32[1,32,128]{2,1,0:T(8,128)S(1)}, s32[1,32,128]{2,1,0:T(8,128)}, u32[]{:S(2)}) copy-start(s32[1,32,128]{2,1,0:T(8,128)} %cells_hbm.1) | copy-start | bytes 49156
  27.8 43.8 %copy-start.38 = (s32[1,32]{1,0:T(1,128)S(1)}, s32[1,32]{1,0:T(1,128)}, u32[]{:S(2)}) copy-start(s32[1,32]{1,0:T(1,128)} %halo_hbm.1) | copy-start | bytes 388
  50.7 1.3 %collective-permute-start = (f32[8,128]{1,0:T(8,128)S(1)}, f32[8,128]{1,0:T(8,128)S(1)}, u32[]{:S(2)}, u32[]{:S(2)}) collective-permute-start(f32[8,128]{1,0:T(8,128)S(1)} %get-tuple-element.199.own_ref), channel_id=1, source_target_pairs={{0,8},{8,0},{16,24},{24,16},{32,40},{40,32},{48,56},{56,48},{64,72... | collective-permute-start | bytes 12296 | tf_op jit(solution)/shard_map/ppermute | solution.py:429
